TPU v7x, 128 devices: a whole 4x4x4 slice. The times are simulated.
128 devices in a mesh: dp: 2 (over z_lo), context: 16 (over x, z_hi, core), tensor: 4 (over y).
Axes of the slice: x: 4, y: 4, z: 4 (z_hi: 2, z_lo: 2; z = z_hi * 2 + z_lo), core: 2. Of those that a mesh axis runs over, the one named last changes fastest.
Arguments:
- hidden_in: bfloat16 [4096, 1024], P(('dp', 'context')), may hold values from -6 to 6
- segments: int32 [2, 2048], P('dp', 'context'), may hold values from 0 to 3, never falling along the last dimension, each value on 1 to 1921 neighbouring positions
- routes: int32 [1, 4096, 8], P(None, ('dp', 'context')), may hold values from 0 to 31, all different within a row; in each aligned block of 128 rows (0 to 127, 128 to 255, ..., all dimensions but the last counted through in order) at most 48 rows name the same one
- norm_attn: bfloat16 [1, 1024], P(None, ('dp', 'context')), may hold values from 0.5 to 1.5
- w_query: bfloat16 [1, 1024, 1024], P(None, ('dp', 'context'), 'tensor'), may hold values from -0.1875 to 0.1875
- w_key: bfloat16 [1, 1024, 512], P(None, ('dp', 'context'), 'tensor'), may hold values from -0.1875 to 0.1875
- w_value: bfloat16 [1, 1024, 512], P(None, ('dp', 'context'), 'tensor'), may hold values from -0.1875 to 0.1875
- w_out: bfloat16 [1, 1024, 1024], P(None, 'tensor', ('dp', 'context')), may hold values from -6 to 6
- norm_ffn: bfloat16 [1, 1024], P(None, ('dp', 'context')), may hold values from 0.5 to 1.5
- w_router: bfloat16 [1, 1024, 32], P(None, ('dp', 'context')), may hold values from -0.09375 to 0.09375
- w_gate: bfloat16 [1, 32, 1024, 512], P(None, 'context', 'dp', 'tensor'), may hold values from -0.1875 to 0.1875
- w_up: bfloat16 [1, 32, 1024, 512], P(None, 'context', 'dp', 'tensor'), may hold values from -0.1875 to 0.1875
- w_down: bfloat16 [1, 32, 512, 1024], P(None, 'context', 'tensor', 'dp'), may hold values from -6 to 6
- cotangent: bfloat16 [4096, 1024], P(('dp', 'context')), may hold values from -6 to 6
Outputs:
- hidden_out: bfloat16 [4096, 1024], P(('dp', 'context'))
- input_grad: float32 [4096, 1024], P(('dp', 'context'))
- norm_attn_grad: float32 [1, 1024], P(None, ('dp', 'context'))
- w_query_grad: float32 [1, 1024, 1024], P(None, ('dp', 'context'), 'tensor')
- w_key_grad: float32 [1, 1024, 512], P(None, ('dp', 'context'), 'tensor')
- w_value_grad: float32 [1, 1024, 512], P(None, ('dp', 'context'), 'tensor')
- w_out_grad: float32 [1, 1024, 1024], P(None, 'tensor', ('dp', 'context'))
- norm_ffn_grad: float32 [1, 1024], P(None, ('dp', 'context'))
- w_router_grad: float32 [1, 1024, 32], P(None, ('dp', 'context'))
- w_gate_grad: float32 [1, 32, 1024, 512], P(None, 'context', 'dp', 'tensor')
- w_up_grad: float32 [1, 32, 1024, 512], P(None, 'context', 'dp', 'tensor')
- w_down_grad: float32 [1, 32, 512, 1024], P(None, 'context', 'tensor', 'dp')
Inputs may be any that keep to these rules, and one draw needn't show every extreme that they name: `segments`: along a sequence the numbers never fall; every number of 0 to 3 occurs; one document of each sequence holds 1921 tokens. `routes`: each row names 8 different experts. Within the 128 rows of one device of one layer no expert is named more than 48 times, a bound that some block reaches.
All inputs are finite; a program needn't handle non-finite values.
Results may differ from a plain program's by a relative error of at most 0.035.
Values may be sent and summed in bfloat16 or wider, within the bound.
A program may use at most 128 MiB of HBM per device.

v0:
```python
import math

import jax
import jax.numpy as jnp
from jax import lax
from jax.sharding import PartitionSpec as P

HEAD = 64


EPS = 1e-06
NEG = -1e30


def for_sending(shard):
    return jax.tree.map(lambda a: a.astype(jnp.bfloat16) if a.dtype == jnp.float32 else a, shard)


def rotary_tables(positions, width):
    half = width // 2
    rates = jnp.exp(jnp.arange(half, dtype=jnp.float32) * (-2.0 * math.log(10000.0) / width))
    angles = positions.astype(jnp.float32)[:, None] * rates[None, :]
    return (jnp.cos(angles), jnp.sin(angles))


def rotate(values, cosine, sine):
    half = values.shape[-1] // 2
    first = values[..., :half]
    second = values[..., half:]
    cosine = cosine[:, None, :]
    sine = sine[:, None, :]
    return jnp.concatenate(
        [first * cosine - second * sine, second * cosine + first * sine], axis=-1
    )


def unrotate(values, cosine, sine):
    half = values.shape[-1] // 2
    first = values[..., :half]
    second = values[..., half:]
    cosine = cosine[:, None, :]
    sine = sine[:, None, :]
    return jnp.concatenate(
        [first * cosine + second * sine, second * cosine - first * sine], axis=-1
    )


def doc_positions(seg_row):
    index = jnp.arange(seg_row.shape[0], dtype=jnp.int32)
    fresh = jnp.concatenate([jnp.ones((1,), jnp.bool_), seg_row[1:] != seg_row[:-1]])
    starts = lax.cummax(jnp.where(fresh, index, jnp.zeros_like(index)), axis=0)
    return index - starts


def route_slots(route_block, experts, capacity):
    flat = route_block.reshape(-1)
    onehot = (flat[:, None] == jnp.arange(experts, dtype=jnp.int32)[None, :]).astype(jnp.int32)
    before = jnp.cumsum(onehot, axis=0) - onehot
    slot = jnp.sum(before * onehot, axis=1)
    return flat * capacity + slot


def slot_tables(slot_of_route, top_count, slots):
    source = jnp.arange(slot_of_route.shape[0], dtype=jnp.int32) // top_count
    owner_rows = jnp.zeros((slots,), jnp.int32).at[slot_of_route].set(source)
    filled = jnp.zeros((slots,), jnp.float32).at[slot_of_route].set(1.0)
    return (owner_rows, filled)


def rms_forward(values, gain):
    inv_scale = lax.rsqrt(jnp.mean(values * values, axis=-1, keepdims=True) + EPS)
    return (values * inv_scale * gain.astype(jnp.float32), inv_scale)


def rms_backward(values, gain, inv_scale, upstream):
    weighted = upstream * gain.astype(jnp.float32)
    inner = jnp.sum(weighted * values, axis=-1, keepdims=True)
    grad_values = inv_scale * weighted - values * inv_scale**3 * inner / values.shape[-1]
    grad_gain = jnp.sum(upstream * values * inv_scale, axis=0)
    return (grad_values, grad_gain)


def fetch_layer(current, norm_attn, w_query, w_key, w_value, w_out, norm_ffn, w_router):
    return (
        lax.all_gather(norm_attn[current], ("dp", "context"), axis=0, tiled=True),
        lax.all_gather(w_query[current], ("dp", "context"), axis=0, tiled=True),
        lax.all_gather(w_key[current], ("dp", "context"), axis=0, tiled=True),
        lax.all_gather(w_value[current], ("dp", "context"), axis=0, tiled=True),
        lax.all_gather(w_out[current], ("dp", "context"), axis=1, tiled=True),
        lax.all_gather(norm_ffn[current], ("dp", "context"), axis=0, tiled=True),
        lax.all_gather(w_router[current], ("dp", "context"), axis=0, tiled=True),
    )


def fetch_experts(current, w_gate, w_up, w_down):
    return (
        lax.all_gather(w_gate[current], "dp", axis=1, tiled=True),
        lax.all_gather(w_up[current], "dp", axis=1, tiled=True),
        lax.all_gather(w_down[current], "dp", axis=2, tiled=True),
    )


def fetch_keys(keys_here, values_here):
    return (
        lax.all_gather(keys_here, "context", axis=0, tiled=True),
        lax.all_gather(values_here, "context", axis=0, tiled=True),
    )


def over_tensor(parts):
    return jax.tree.map(
        lambda part: part.astype(jnp.float32), lax.psum(for_sending(parts), "tensor")
    )


def route_rows(buffer):
    return lax.all_to_all(buffer, "context", split_axis=0, concat_axis=0, tiled=True)


def experts_forward(inputs, gate_map, up_map, down_map):
    gate_pre = jnp.einsum("secd,edf->secf", inputs, gate_map, preferred_element_type=jnp.float32)
    up_pre = jnp.einsum("secd,edf->secf", inputs, up_map, preferred_element_type=jnp.float32)
    inner = (jax.nn.silu(gate_pre) * up_pre).astype(jnp.bfloat16)
    result = jnp.einsum(
        "secf,efd->secd", inner, down_map, preferred_element_type=jnp.float32
    ).astype(jnp.bfloat16)
    return (result, (gate_pre, up_pre, inner))


def experts_backward(inputs, gate_map, up_map, down_map, kept_parts, upstream):
    gate_pre, up_pre, inner = kept_parts
    grad_inner = jnp.einsum(
        "secd,efd->secf", upstream, down_map, preferred_element_type=jnp.float32
    )
    grad_down = jnp.einsum("secf,secd->efd", inner, upstream, preferred_element_type=jnp.float32)
    sigma = jax.nn.sigmoid(gate_pre)
    grad_gate = (grad_inner * up_pre * sigma * (1.0 + gate_pre * (1.0 - sigma))).astype(
        jnp.bfloat16
    )
    grad_up = (grad_inner * gate_pre * sigma).astype(jnp.bfloat16)
    grad_gate_map = jnp.einsum(
        "secd,secf->edf", inputs, grad_gate, preferred_element_type=jnp.float32
    )
    grad_up_map = jnp.einsum("secd,secf->edf", inputs, grad_up, preferred_element_type=jnp.float32)
    grad_inputs = jnp.einsum(
        "secf,edf->secd", grad_gate, gate_map, preferred_element_type=jnp.float32
    )
    grad_inputs = grad_inputs + jnp.einsum(
        "secf,edf->secd", grad_up, up_map, preferred_element_type=jnp.float32
    )
    return (grad_inputs.astype(jnp.bfloat16), grad_gate_map, grad_up_map, grad_down)


def per_device(
    hidden_in,
    segments,
    routes,
    norm_attn,
    w_query,
    w_key,
    w_value,
    w_out,
    norm_ffn,
    w_router,
    w_gate,
    w_up,
    w_down,
    cotangent,
):
    rows_here, model_width = hidden_in.shape
    contexts = lax.axis_size("context")
    context_pos = lax.axis_index("context")
    layer_count = w_query.shape[0]
    top_count = routes.shape[2]
    experts = w_router.shape[2]
    local_experts = w_gate.shape[1]
    heads_here = w_query.shape[2] // HEAD
    kv_here = w_key.shape[2] // HEAD
    group_size = heads_here // kv_here
    capacity = min(rows_here, 3 * rows_here * top_count // (2 * experts))
    slots = experts * capacity
    seg_all = lax.all_gather(segments, "context", axis=1, tiled=True)[0]
    seq_len = seg_all.shape[0]
    start_row = context_pos * rows_here
    positions = lax.dynamic_slice_in_dim(doc_positions(seg_all), start_row, rows_here, 0)
    seg_here = lax.dynamic_slice_in_dim(seg_all, start_row, rows_here, 0)
    cosine, sine = rotary_tables(positions, HEAD)
    query_index = start_row + jnp.arange(rows_here, dtype=jnp.int32)
    key_index = jnp.arange(seq_len, dtype=jnp.int32)
    allowed = (seg_here[:, None] == seg_all[None, :]) & (key_index[None, :] <= query_index[:, None])
    expert_ids = jnp.arange(experts, dtype=jnp.int32)

    def to_experts(rows):
        arrived_rows = route_rows(rows.reshape(contexts, local_experts * capacity, model_width))
        return arrived_rows.reshape(contexts, local_experts, capacity, model_width)

    def from_experts(results):
        back_rows = route_rows(results.reshape(contexts, local_experts * capacity, model_width))
        return back_rows.reshape(slots, model_width).astype(jnp.float32)

    residual = hidden_in.astype(jnp.float32)
    current = 0
    attn_gain, query_map, key_map, value_map, out_map, ffn_gain, router_map = fetch_layer(
        current, norm_attn, w_query, w_key, w_value, w_out, norm_ffn, w_router
    )
    gate_map, up_map, down_map = fetch_experts(current, w_gate, w_up, w_down)
    normed_f, scale_one = rms_forward(residual, attn_gain)
    normed = normed_f.astype(jnp.bfloat16)
    queries = rotate(
        jnp.dot(normed, query_map, preferred_element_type=jnp.float32).reshape(
            rows_here, heads_here, HEAD
        ),
        cosine,
        sine,
    )
    queries = (queries * 0.125).astype(jnp.bfloat16).reshape(rows_here, kv_here, group_size, HEAD)
    keys_here = rotate(
        jnp.dot(normed, key_map, preferred_element_type=jnp.float32).reshape(
            rows_here, kv_here, HEAD
        ),
        cosine,
        sine,
    ).astype(jnp.bfloat16)
    values_here = (
        jnp.dot(normed, value_map, preferred_element_type=jnp.float32)
        .astype(jnp.bfloat16)
        .reshape(rows_here, kv_here, HEAD)
    )
    keys_all, values_all = fetch_keys(keys_here, values_here)
    scores = jnp.einsum("qhgd,khd->hgqk", queries, keys_all, preferred_element_type=jnp.float32)
    scores = jnp.where(allowed, scores, NEG)
    top_score = jnp.max(scores, axis=-1, keepdims=True)
    expo = jnp.where(allowed, jnp.exp(scores - top_score), 0.0)
    total = jnp.sum(expo, axis=-1, keepdims=True)
    log_total = top_score + jnp.log(total)
    weights = (expo / total).astype(jnp.bfloat16)
    attended = jnp.einsum("hgqk,khd->qhgd", weights, values_all, preferred_element_type=jnp.float32)
    attended_low = attended.reshape(rows_here, heads_here * HEAD).astype(jnp.bfloat16)
    hidden = residual + over_tensor(
        jnp.dot(attended_low, out_map, preferred_element_type=jnp.float32)
    )
    normed_two_f, scale_two = rms_forward(hidden, ffn_gain)
    normed_two = normed_two_f.astype(jnp.bfloat16)
    logits = jnp.dot(normed_two, router_map, preferred_element_type=jnp.float32)
    probs = jax.nn.softmax(logits, axis=-1)
    chosen = (routes[current][:, :, None] == expert_ids[None, None, :]).astype(jnp.float32)
    gate_values = jnp.sum(chosen * probs[:, None, :], axis=-1)
    slot_of_route = route_slots(routes[current], experts, capacity)
    token_of_slot, filled = slot_tables(slot_of_route, top_count, slots)
    slot_gate = jnp.zeros((slots,), jnp.float32).at[slot_of_route].set(gate_values.reshape(-1))
    outgoing = jnp.where(
        filled[:, None] > 0.5, normed_two[token_of_slot], jnp.zeros((), jnp.bfloat16)
    )
    arrived = to_experts(outgoing)
    produced, kept_parts = experts_forward(arrived, gate_map, up_map, down_map)
    returned = from_experts(produced)
    picked = returned[slot_of_route].reshape(rows_here, top_count, model_width)
    weighted_sum = jnp.sum(gate_values[:, :, None] * picked, axis=1)
    expert_out = over_tensor(weighted_sum)
    saved_layers = [
        (
            residual,
            scale_one,
            normed,
            queries,
            keys_all,
            values_all,
            log_total,
            attended,
            attended_low,
            hidden,
            scale_two,
            normed_two,
            probs,
            chosen,
            slot_of_route,
            token_of_slot,
            slot_gate,
            arrived,
            kept_parts,
            picked,
        )
    ]
    residual = hidden + expert_out
    hidden_out = residual.astype(jnp.bfloat16)
    gradient = cotangent.astype(jnp.float32)
    (
        grads_attn_gain,
        grads_query,
        grads_key,
        grads_value,
        grads_out,
        grads_ffn_gain,
        grads_router,
    ) = ([], [], [], [], [], [], [])
    grads_gate, grads_up, grads_down = ([], [], [])
    for current in reversed(range(layer_count)):
        (
            layer_input,
            scale_one,
            normed,
            queries,
            keys_all,
            values_all,
            log_total,
            attended,
            attended_low,
            hidden,
            scale_two,
            normed_two,
            probs,
            chosen,
            slot_of_route,
            token_of_slot,
            slot_gate,
            arrived,
            kept_parts,
            picked,
        ) = saved_layers[current]
        attn_gain, query_map, key_map, value_map, out_map, ffn_gain, router_map = fetch_layer(
            current, norm_attn, w_query, w_key, w_value, w_out, norm_ffn, w_router
        )
        gate_map, up_map, down_map = fetch_experts(current, w_gate, w_up, w_down)
        grad_gate_part = jnp.sum(picked * gradient[:, None, :], axis=-1)
        upstream = (slot_gate[:, None] * gradient[token_of_slot]).astype(jnp.bfloat16)
        arrived_grad = to_experts(upstream)
        grad_inputs, grad_gate_map, grad_up_map, grad_down_map = experts_backward(
            arrived, gate_map, up_map, down_map, kept_parts, arrived_grad
        )
        grad_rows = from_experts(grad_inputs)
        grad_gate_map, grad_up_map, grad_down_map = (
            lax.psum_scatter(
                grad_gate_map.astype(jnp.bfloat16), "dp", scatter_dimension=1, tiled=True
            ).astype(jnp.float32),
            lax.psum_scatter(
                grad_up_map.astype(jnp.bfloat16), "dp", scatter_dimension=1, tiled=True
            ).astype(jnp.float32),
            lax.psum_scatter(
                grad_down_map.astype(jnp.bfloat16), "dp", scatter_dimension=2, tiled=True
            ).astype(jnp.float32),
        )
        grads_gate.append(grad_gate_map)
        grads_up.append(grad_up_map)
        grads_down.append(grad_down_map)
        grad_norm_part = jnp.sum(
            grad_rows[slot_of_route].reshape(rows_here, top_count, model_width), axis=1
        )
        grad_norm_experts, grad_gates = over_tensor((grad_norm_part, grad_gate_part))
        grad_probs = jnp.sum(chosen * grad_gates[:, :, None], axis=1)
        grad_logits = (
            probs * (grad_probs - jnp.sum(probs * grad_probs, axis=-1, keepdims=True))
        ).astype(jnp.bfloat16)
        grads_router.append(
            jnp.einsum("td,te->de", normed_two, grad_logits, preferred_element_type=jnp.float32)
        )
        grad_normed_two = grad_norm_experts + jnp.einsum(
            "te,de->td", grad_logits, router_map, preferred_element_type=jnp.float32
        )
        grad_from_ffn, grad_ffn_gain = rms_backward(hidden, ffn_gain, scale_two, grad_normed_two)
        grads_ffn_gain.append(grad_ffn_gain)
        grad_hidden = gradient + grad_from_ffn
        grad_attn = grad_hidden.astype(jnp.bfloat16)
        grads_out.append(
            jnp.einsum("tc,td->cd", attended_low, grad_attn, preferred_element_type=jnp.float32)
        )
        grad_attended = jnp.einsum(
            "td,cd->tc", grad_attn, out_map, preferred_element_type=jnp.float32
        ).astype(jnp.bfloat16)
        grad_attended = grad_attended.reshape(rows_here, kv_here, group_size, HEAD)
        row_delta = jnp.einsum("qhgd,qhgd->hgq", grad_attended.astype(jnp.float32), attended)
        scores = jnp.einsum("qhgd,khd->hgqk", queries, keys_all, preferred_element_type=jnp.float32)
        weights = jnp.where(allowed, jnp.exp(scores - log_total), 0.0)
        grad_weights = jnp.einsum(
            "qhgd,khd->hgqk", grad_attended, values_all, preferred_element_type=jnp.float32
        )
        grad_scores = (weights * (grad_weights - row_delta[..., None])).astype(jnp.bfloat16)
        grad_queries = jnp.einsum(
            "hgqk,khd->qhgd", grad_scores, keys_all, preferred_element_type=jnp.float32
        )
        grad_keys_all = jnp.einsum(
            "hgqk,qhgd->khd", grad_scores, queries, preferred_element_type=jnp.float32
        )
        grad_values_all = jnp.einsum(
            "hgqk,qhgd->khd",
            weights.astype(jnp.bfloat16),
            grad_attended,
            preferred_element_type=jnp.float32,
        )
        grad_keys, grad_values = (
            lax.psum_scatter(
                grad_keys_all.astype(jnp.bfloat16), "context", scatter_dimension=0, tiled=True
            ).astype(jnp.float32),
            lax.psum_scatter(
                grad_values_all.astype(jnp.bfloat16), "context", scatter_dimension=0, tiled=True
            ).astype(jnp.float32),
        )
        grad_query_lin = (
            (unrotate(grad_queries.reshape(rows_here, heads_here, HEAD), cosine, sine) * 0.125)
            .astype(jnp.bfloat16)
            .reshape(rows_here, heads_here * HEAD)
        )
        grad_key_lin = (
            unrotate(grad_keys, cosine, sine)
            .astype(jnp.bfloat16)
            .reshape(rows_here, kv_here * HEAD)
        )
        grad_value_lin = grad_values.astype(jnp.bfloat16).reshape(rows_here, kv_here * HEAD)
        grads_query.append(
            jnp.einsum("td,tc->dc", normed, grad_query_lin, preferred_element_type=jnp.float32)
        )
        grads_key.append(
            jnp.einsum("td,tc->dc", normed, grad_key_lin, preferred_element_type=jnp.float32)
        )
        grads_value.append(
            jnp.einsum("td,tc->dc", normed, grad_value_lin, preferred_element_type=jnp.float32)
        )
        grad_normed_part = jnp.einsum(
            "tc,dc->td", grad_query_lin, query_map, preferred_element_type=jnp.float32
        )
        grad_normed_part = grad_normed_part + jnp.einsum(
            "tc,dc->td", grad_key_lin, key_map, preferred_element_type=jnp.float32
        )
        grad_normed_part = grad_normed_part + jnp.einsum(
            "tc,dc->td", grad_value_lin, value_map, preferred_element_type=jnp.float32
        )
        grad_normed = over_tensor(grad_normed_part)
        grad_from_attn, grad_attn_gain = rms_backward(
            layer_input, attn_gain, scale_one, grad_normed
        )
        grads_attn_gain.append(grad_attn_gain)
        gradient = grad_hidden + grad_from_attn
    shard_lists = ([], [], [], [], [], [], [])
    current = 0
    back = layer_count - 1 - current
    pieces = (
        lax.psum_scatter(
            grads_attn_gain[back].astype(jnp.bfloat16),
            ("dp", "context"),
            scatter_dimension=0,
            tiled=True,
        ).astype(jnp.float32),
        lax.psum_scatter(
            grads_query[back].astype(jnp.bfloat16),
            ("dp", "context"),
            scatter_dimension=0,
            tiled=True,
        ).astype(jnp.float32),
        lax.psum_scatter(
            grads_key[back].astype(jnp.bfloat16), ("dp", "context"), scatter_dimension=0, tiled=True
        ).astype(jnp.float32),
        lax.psum_scatter(
            grads_value[back].astype(jnp.bfloat16),
            ("dp", "context"),
            scatter_dimension=0,
            tiled=True,
        ).astype(jnp.float32),
        lax.psum_scatter(
            grads_out[back].astype(jnp.bfloat16), ("dp", "context"), scatter_dimension=1, tiled=True
        ).astype(jnp.float32),
        lax.psum_scatter(
            grads_ffn_gain[back].astype(jnp.bfloat16),
            ("dp", "context"),
            scatter_dimension=0,
            tiled=True,
        ).astype(jnp.float32),
        lax.psum_scatter(
            grads_router[back].astype(jnp.bfloat16),
            ("dp", "context"),
            scatter_dimension=0,
            tiled=True,
        ).astype(jnp.float32),
    )
    for number in range(7):
        shard_lists[number].append(pieces[number])
    stacked = [jnp.stack(items) for items in shard_lists]
    gate_stack = jnp.stack(grads_gate[::-1])
    up_stack = jnp.stack(grads_up[::-1])
    down_stack = jnp.stack(grads_down[::-1])
    return (
        hidden_out,
        gradient,
        stacked[0],
        stacked[1],
        stacked[2],
        stacked[3],
        stacked[4],
        stacked[5],
        stacked[6],
        gate_stack,
        up_stack,
        down_stack,
    )


def solution(mesh):
    in_specs = (
        P(("dp", "context"), None),
        P("dp", "context"),
        P(None, ("dp", "context"), None),
        P(None, ("dp", "context")),
        P(None, ("dp", "context"), "tensor"),
        P(None, ("dp", "context"), "tensor"),
        P(None, ("dp", "context"), "tensor"),
        P(None, "tensor", ("dp", "context")),
        P(None, ("dp", "context")),
        P(None, ("dp", "context"), None),
        P(None, "context", "dp", "tensor"),
        P(None, "context", "dp", "tensor"),
        P(None, "context", "tensor", "dp"),
        P(("dp", "context"), None),
    )
    out_specs = (
        P(("dp", "context"), None),
        P(("dp", "context"), None),
        P(None, ("dp", "context")),
        P(None, ("dp", "context"), "tensor"),
        P(None, ("dp", "context"), "tensor"),
        P(None, ("dp", "context"), "tensor"),
        P(None, "tensor", ("dp", "context")),
        P(None, ("dp", "context")),
        P(None, ("dp", "context"), None),
        P(None, "context", "dp", "tensor"),
        P(None, "context", "dp", "tensor"),
        P(None, "context", "tensor", "dp"),
    )
    return jax.shard_map(
        per_device, mesh=mesh, in_specs=in_specs, out_specs=out_specs, check_vma=False
    )
```

profile of v0, /device:TPU:0, one launch (start us, length us, event | category | flops | bytes accessed | tf_op | source)
XLA Modules:
  0.0 1609.7 jit_solution(13902282638878139753)
XLA Ops:
  12.7 68.5 %all-reduce.5 = (bf16[1024]{0:T(1024)(128)(2,1)S(1)}, bf16[1024]{0:T(1024)(128)(2,1)S(1)}) all-reduce(bf16[1024]{0:T(1024)(128)(2,1)S(1)} %dynamic-update-slice, bf16[1024]{0:T(1024)(128)(2,1)S(1)} %dynamic-update-slice.1), channel_id=2, replica_groups=mesh['dp'=2,'context'=16,'tensor'=4] {'dp','context'}, use_global_device_ids=true, to_apply=%add | all-reduce | flops 2048 | bytes 8192
  81.1 19.1 %all_gather.52 = s32[1,2048]{1,0:T(1,128)S(1)} all-gather(s32[1,128]{1,0:T(1,128)} %param.15), channel_id=1, replica_groups=mesh['dp'=2,'context'=16,'tensor'=4] {'context'}, dimensions={1}, use_global_device_ids=true | all-gather | bytes 8704 | tf_op jit(solution)/shard_map/all_gather | solution.py:182
  101.1 39.5 %all-gather.2 = bf16[1,1024,128]{2,1,0:T(8,128)(2,1)S(1)} all-gather(bf16[1,32,128]{2,1,0:T(8,128)(2,1)} %param.19), channel_id=4, replica_groups=mesh['dp'=2,'context'=16,'tensor'=4] {'dp','context'}, dimensions={1}, use_global_device_ids=true | all-gather | bytes 270336 | tf_op jit(solution)/shard_map/all_gather | solution.py:87
  140.6 36.5 %all-gather.1 = bf16[1,1024,128]{2,1,0:T(8,128)(2,1)S(1)} all-gather(bf16[1,32,128]{2,1,0:T(8,128)(2,1)} %param.20), channel_id=3, replica_groups=mesh['dp'=2,'context'=16,'tensor'=4] {'dp','context'}, dimensions={1}, use_global_device_ids=true | all-gather | bytes 270336 | tf_op jit(solution)/shard_map/all_gather | solution.py:88
  179.7 23.5 %all_gather.51 = bf16[2048,2,64]{0,2,1:T(8,128)(2,1)S(1)} all-gather(bf16[128,2,64]{0,2,1:T(8,128)(2,1)S(1)} %bitcast.307), channel_id=1, replica_groups=mesh['dp'=2,'context'=16,'tensor'=4] {'context'}, dimensions={0}, use_global_device_ids=true | all-gather | bytes 557056 | tf_op jit(solution)/shard_map/all_gather | solution.py:106
  203.5 20.7 %all_gather.54 = bf16[2048,2,64]{0,2,1:T(8,128)(2,1)S(1)} all-gather(bf16[128,2,64]{0,2,1:T(8,128)(2,1)S(1)} %pad_maximum_fusion), channel_id=1, replica_groups=mesh['dp'=2,'context'=16,'tensor'=4] {'context'}, dimensions={0}, use_global_device_ids=true | all-gather | bytes 557056 | tf_op jit(solution)/shard_map/all_gather | solution.py:105
  224.2 40.2 %all-gather.3 = bf16[1,1024,256]{2,1,0:T(8,128)(2,1)S(1)} all-gather(bf16[1,32,256]{2,1,0:T(8,128)(2,1)} %param.18), channel_id=5, replica_groups=mesh['dp'=2,'context'=16,'tensor'=4] {'dp','context'}, dimensions={1}, use_global_device_ids=true | all-gather | bytes 540672 | tf_op jit(solution)/shard_map/all_gather | solution.py:86
  264.8 37.1 %all-gather.4 = bf16[1,256,1024]{1,2,0:T(8,128)(2,1)S(1)} all-gather(bf16[1,256,32]{1,2,0:T(8,128)(2,1)S(1)} %copy-done.38), channel_id=6, replica_groups=mesh['dp'=2,'context'=16,'tensor'=4] {'dp','context'}, dimensions={2}, use_global_device_ids=true | all-gather | bytes 540672 | tf_op jit(solution)/shard_map/all_gather | solution.py:89
  307.4 9.0 reduce-window.19
  317.0 4.3 scatter_custom_fusion.1
  321.3 4.3 scatter_custom_fusion
  325.7 22.0 %all-reduce.11.cloned.1.call-done = bf16[128,1024]{1,0:T(8,128)(2,1)} async-done(((bf16[128,1024]{1,0:T(8,128)(2,1)}), bf16[128,1024]{1,0:T(8,128)(2,1)}) %all-reduce.11.cloned.1.call-update) | async-done | bytes 262160 | tf_op jit(solution)/shard_map/psum | solution.py:112
  350.5 5.8 gather_fusion
  359.7 7.3 all-to-all-start
  367.1 5.8 gather_fusion.2
  372.9 68.9 %all-gather.6 = bf16[1,1024,32]{2,1,0:T(8,128)(2,1)S(1)} all-gather(bf16[1,32,32]{2,1,0:T(8,128)(2,1)S(1)} %copy-done.47), channel_id=8, replica_groups=mesh['dp'=2,'context'=16,'tensor'=4] {'dp','context'}, dimensions={1}, use_global_device_ids=true | all-gather | bytes 67584 | tf_op jit(solution)/shard_map/all_gather | solution.py:91
  442.8 4.3 scatter_custom_fusion.2
  447.2 4.9 multiply_convert_fusion
  452.1 4.6 all-to-all-start.2
  456.8 31.7 %all-gather.7 = bf16[1,2,1024,128]{3,2,1,0:T(8,128)(2,1)S(1)} all-gather(bf16[1,2,512,128]{3,2,1,0:T(8,128)(2,1)S(1)} %copy-done.20), channel_id=9, replica_groups=mesh['dp'=2,'context'=16,'tensor'=4] {'dp'}, dimensions={2}, use_global_device_ids=true | all-gather | bytes 786432 | tf_op jit(solution)/shard_map/all_gather | solution.py:97
  488.5 14.4 all-gather.8
  502.9 9.9 all-gather.9
  520.3 4.4 multiply_convert_fusion.1
  528.7 9.2 all-to-all-start.1
  542.1 36.3 %all-to-all-done.1 = bf16[16,96,1024]{2,1,0:T(8,128)(2,1)} async-done(((bf16[16,96,1024]{2,1,0:T(8,128)(2,1)}), bf16[16,96,1024]{2,1,0:T(8,128)(2,1)}, u32[]{:S(2)}, u32[]{:S(2)}) %all-to-all-start.1) | async-done | bytes 3145760 | tf_op jit(solution)/shard_map/all_to_all | solution.py:117
  578.5 8.7 all-to-all-start.3
  588.1 5.3 bitcast_convert_fusion.1
  593.4 9.3 gather_fusion.1
  602.7 4.5 fusion.3
  607.2 9.4 psum.38
  616.6 11.2 all-to-all-done.3
  627.8 5.3 bitcast_convert_fusion
  633.1 9.2 gather_fusion.3
  646.5 43.9 %all-reduce.13.cloned.1.call-done = bf16[128,1024]{1,0:T(8,128)(2,1)} async-done(((bf16[128,1024]{1,0:T(8,128)(2,1)}), bf16[128,1024]{1,0:T(8,128)(2,1)}) %all-reduce.13.cloned.1.call-update) | async-done | bytes 262160 | tf_op jit(solution)/shard_map/psum | solution.py:112
  710.0 4.1 fusion.41
  714.5 4.1 fusion.40
  725.9 40.6 %reduce-scatter.31.cloned.1.call-done = bf16[128,128]{1,0:T(8,128)(2,1)} async-done(((bf16[2048,128]{1,0:T(8,128)(2,1)}), bf16[128,128]{1,0:T(8,128)(2,1)}) %reduce-scatter.31.cloned.1.call-update) | async-done | bytes 32784
  768.6 66.3 %reduce-scatter.33.cloned.1.call-done = bf16[128,128]{1,0:T(8,128)(2,1)} async-done(((bf16[2048,128]{1,0:T(8,128)(2,1)}), bf16[128,128]{1,0:T(8,128)(2,1)}) %reduce-scatter.33.cloned.1.call-update) | async-done | bytes 32784 | tf_op jit(solution)/shard_map/reshape | solution.py:407
  836.8 17.0 %reduce-scatter.29.cloned.1.call-done = bf16[2,128,512]{2,1,0:T(8,128)(2,1)} async-done(((bf16[2,128,1024]{2,1,0:T(8,128)(2,1)}), bf16[2,128,512]{2,1,0:T(8,128)(2,1)}) %reduce-scatter.29.cloned.1.call-update) | async-done | bytes 262160 | tf_op jit(solution)/shard_map/reduce_scatter | solution.py:338
  855.6 18.7 %reduce-scatter.27.cloned.1.call-done = bf16[2,512,128]{2,1,0:T(8,128)(2,1)} async-done(((bf16[2,1024,128]{2,1,0:T(8,128)(2,1)}), bf16[2,512,128]{2,1,0:T(8,128)(2,1)}) %reduce-scatter.27.cloned.1.call-update) | async-done | bytes 262160 | tf_op jit(solution)/shard_map/reduce_scatter | solution.py:335
  878.0 16.8 %reduce-scatter.25.cloned.1.call-done = bf16[2,512,128]{2,1,0:T(8,128)(2,1)} async-done(((bf16[2,1024,128]{2,1,0:T(8,128)(2,1)}), bf16[2,512,128]{2,1,0:T(8,128)(2,1)}) %reduce-scatter.25.cloned.1.call-update) | async-done | bytes 262160 | tf_op jit(solution)/shard_map/reduce_scatter | solution.py:332
  896.6 133.7 %reduce-scatter.23.cloned.1.call-done = bf16[32,32]{1,0:T(8,128)(2,1)} async-done(((bf16[1024,32]{1,0:T(8,128)(2,1)}), bf16[32,32]{1,0:T(8,128)(2,1)}) %reduce-scatter.23.cloned.1.call-update) | async-done | bytes 2064 | tf_op jit(solution)/shard_map/reduce_scatter | solution.py:466
  1032.7 128.3 %reduce-scatter.21.cloned.1.call-done = bf16[256,32]{0,1:T(8,128)(2,1)} async-done(((bf16[256,1024]{0,1:T(8,128)(2,1)}), bf16[256,32]{0,1:T(8,128)(2,1)}) %reduce-scatter.21.cloned.1.call-update) | async-done | bytes 16400 | tf_op jit(solution)/shard_map/reduce_scatter | solution.py:457
  1162.3 129.6 %reduce-scatter.15.cloned.1.call-done = bf16[32,256]{1,0:T(8,128)(2,1)} async-done(((bf16[1024,256]{1,0:T(8,128)(2,1)}), bf16[32,256]{1,0:T(8,128)(2,1)}) %reduce-scatter.15.cloned.1.call-update) | async-done | bytes 16400 | tf_op jit(solution)/shard_map/reduce_scatter | solution.py:442
  1293.2 41.1 %all-reduce.15.cloned.1.call-done = (bf16[128,1024]{1,0:T(8,128)(2,1)}, bf16[128,1024]{1,0:T(8,128)(2,1)}) async-done(((bf16[128,1024]{1,0:T(8,128)(2,1)}, bf16[128,1024]{1,0:T(8,128)(2,1)}), (bf16[128,1024]{1,0:T(8,128)(2,1)}, bf16[128,1024]{1,0:T(8,128)(2,1)})) %all-reduce.15.cloned.1.call-update) | async-done | bytes 524304 | tf_op jit(solution)/shard_map/psum | solution.py:112
  1335.4 65.5 %all-reduce.4 = (bf16[1024]{0:T(1024)(128)(2,1)S(1)}, bf16[1024]{0:T(1024)(128)(2,1)S(1)}) all-reduce(bf16[1024]{0:T(1024)(128)(2,1)S(1)} %get-tuple-element.16, bf16[1024]{0:T(1024)(128)(2,1)S(1)} %get-tuple-element.14), channel_id=14, replica_groups=mesh['dp'=2,'context'=16,'tensor'=4] {'dp','context'}, use_global_device_ids=true, to_apply=%region_30.31.clone | all-reduce | flops 2048 | bytes 8192
  1401.5 67.3 %reduce-scatter.19.cloned.1.call-done = bf16[32,128]{1,0:T(8,128)(2,1)} async-done(((bf16[1024,128]{1,0:T(8,128)(2,1)}), bf16[32,128]{1,0:T(8,128)(2,1)}) %reduce-scatter.19.cloned.1.call-update) | async-done | bytes 8208 | tf_op jit(solution)/shard_map/reduce_scatter | solution.py:451
  1470.1 129.2 %reduce-scatter.17.cloned.1.call-done = bf16[32,128]{1,0:T(8,128)(2,1)} async-done(((bf16[1024,128]{1,0:T(8,128)(2,1)}), bf16[32,128]{1,0:T(8,128)(2,1)}) %reduce-scatter.17.cloned.1.call-update) | async-done | bytes 8208 | tf_op jit(solution)/shard_map/reduce_scatter | solution.py:448
  (251 shorter events, 91.7 us)
Async XLA Ops:
  7.2 257.2 %copy-start = (bf16[128,1024]{1,0:T(8,128)(2,1)S(1)}, bf16[128,1024]{1,0:T(8,128)(2,1)}, u32[]{:S(2)}) copy-start(bf16[128,1024]{1,0:T(8,128)(2,1)} %param.14) | copy-start | bytes 786436
  7.2 257.6 %copy-start.38 = (bf16[1,256,32]{1,2,0:T(8,128)(2,1)S(1)}, bf16[1,256,32]{1,2,0:T(8,128)(2,1)}, u32[]{:S(2)}) copy-start(bf16[1,256,32]{1,2,0:T(8,128)(2,1)} %param.21) | copy-start | bytes 49156
  7.2 340.6 %all-reduce.11.cloned.1.call-start = ((), (), s32[]{:S(2)}) async-start(), calls=%async_computation.14 | async-start | bytes 524288 | tf_op jit(solution)/shard_map/psum | solution.py:112
  9.0 294.0 %copy-start.36 = (f32[128]{0:T(128)}, f32[128]{0:T(128)S(1)}, u32[]{:S(2)}) copy-start(f32[128]{0:T(128)S(1)} %get-tuple-element.42) | copy-start | bytes 1540
  81.1 221.9 %copy-start.25 = (f32[1024]{0:T(1024)}, f32[1024]{0:T(1024)S(1)}, u32[]{:S(2)}) copy-start(f32[1024]{0:T(1024)S(1)} %convert_element_type.267) | copy-start | bytes 12292
  140.6 62.8 %copy-start.7 = (bf16[1,1024,128]{2,1,0:T(8,128)(2,1)}, bf16[1,1024,128]{2,1,0:T(8,128)(2,1)S(1)}, u32[]{:S(2)}) copy-start(bf16[1,1024,128]{2,1,0:T(8,128)(2,1)S(1)} %all-gather.2) | copy-start | bytes 786436
  177.1 26.4 %copy-start.6 = (bf16[1,1024,128]{2,1,0:T(8,128)(2,1)}, bf16[1,1024,128]{2,1,0:T(8,128)(2,1)S(1)}, u32[]{:S(2)}) copy-start(bf16[1,1024,128]{2,1,0:T(8,128)(2,1)S(1)} %all-gather.1) | copy-start | bytes 786436
  203.2 100.7 %copy-start.12 = (bf16[2048,2,64]{0,2,1:T(8,128)(2,1)}, bf16[2048,2,64]{0,2,1:T(8,128)(2,1)S(1)}, u32[]{:S(2)}) copy-start(bf16[2048,2,64]{0,2,1:T(8,128)(2,1)S(1)} %all_gather.51) | copy-start | bytes 1572868
  203.4 99.7 %copy-start.13 = (f32[128,32]{0,1:T(8,128)}, f32[128,32]{0,1:T(8,128)S(1)}, u32[]{:S(2)}) copy-start(f32[128,32]{0,1:T(8,128)S(1)} %get-tuple-element.37) | copy-start | bytes 49156
  203.4 99.7 %copy-start.15 = (f32[128,32]{0,1:T(8,128)}, f32[128,32]{0,1:T(8,128)S(1)}, u32[]{:S(2)}) copy-start(f32[128,32]{0,1:T(8,128)S(1)} %get-tuple-element.38) | copy-start | bytes 49156
  224.2 78.0 %copy-start.4 = (bf16[2048,2,64]{0,2,1:T(8,128)(2,1)}, bf16[2048,2,64]{0,2,1:T(8,128)(2,1)S(1)}, u32[]{:S(2)}) copy-start(bf16[2048,2,64]{0,2,1:T(8,128)(2,1)S(1)} %all_gather.54) | copy-start | bytes 1572868
  264.4 37.9 %copy-start.3 = (bf16[1,1024,256]{2,1,0:T(8,128)(2,1)}, bf16[1,1024,256]{2,1,0:T(8,128)(2,1)S(1)}, u32[]{:S(2)}) copy-start(bf16[1,1024,256]{2,1,0:T(8,128)(2,1)S(1)} %all-gather.3) | copy-start | bytes 1572868
  305.8 50.5 %copy-start.23 = (bf16[128,2,2,64]{0,3,2,1:T(8,128)(2,1)}, bf16[128,2,2,64]{0,3,2,1:T(8,128)(2,1)S(1)}, u32[]{:S(2)}) copy-start(bf16[128,2,2,64]{0,3,2,1:T(8,128)(2,1)S(1)} %get-tuple-element.47) | copy-start | bytes 196612
  307.2 49.1 %copy-start.30 = (f32[1024]{0:T(1024)}, f32[1024]{0:T(1024)S(1)}, u32[]{:S(2)}) copy-start(f32[1024]{0:T(1024)S(1)} %convert_element_type.268) | copy-start | bytes 12292
  316.9 125.9 %copy-start.39 = (s32[1024,1]{0,1:T(1,128)}, s32[1024,1]{0,1:T(1,128)S(1)}, u32[]{:S(2)}) copy-start(s32[1024,1]{0,1:T(1,128)S(1)} %compare_select_fusion) | copy-start | bytes 12292
  359.7 92.4 %all-to-all-start = ((bf16[16,96,1024]{2,1,0:T(8,128)(2,1)}), bf16[16,96,1024]{2,1,0:T(8,128)(2,1)}, u32[]{:S(2)}, u32[]{:S(2)}) async-start(bf16[16,96,1024]{2,1,0:T(8,128)(2,1)} %broadcast_select_fusion), calls=%async_computation | async-start | bytes 6291456 | tf_op jit(solution)/shard_map/all_to_all | solution.py:117
  442.7 9.4 copy-start.10
  452.1 36.4 %copy-start.21 = (bf16[1,2,512,128]{3,2,1,0:T(8,128)(2,1)S(1)}, bf16[1,2,512,128]{3,2,1,0:T(8,128)(2,1)}, u32[]{:S(2)}) copy-start(bf16[1,2,512,128]{3,2,1,0:T(8,128)(2,1)} %param.25) | copy-start | bytes 786436
  452.1 68.2 %all-to-all-start.2 = ((bf16[16,96,1024]{2,1,0:T(8,128)(2,1)}), bf16[16,96,1024]{2,1,0:T(8,128)(2,1)}, u32[]{:S(2)}, u32[]{:S(2)}) async-start(bf16[16,96,1024]{2,1,0:T(8,128)(2,1)} %multiply_convert_fusion), calls=%async_computation.2 | async-start | bytes 6291456 | tf_op jit(solution)/shard_map/all_to_all | solution.py:117
  528.7 9.3 copy-start.17
  528.7 49.8 %all-to-all-start.1 = ((bf16[16,96,1024]{2,1,0:T(8,128)(2,1)}), bf16[16,96,1024]{2,1,0:T(8,128)(2,1)}, u32[]{:S(2)}, u32[]{:S(2)}) async-start(bf16[16,96,1024]{2,1,0:T(8,128)(2,1)} %bitcast.283), calls=%async_computation.1 | async-start | bytes 6291456 | tf_op jit(solution)/shard_map/all_to_all | solution.py:117
  542.1 45.4 %copy-start.35 = (f32[2,2,128]{2,1,0:T(2,128)S(1)}, f32[2,2,128]{2,1,0:T(2,128)}, u32[]{:S(2)}) copy-start(f32[2,2,128]{2,1,0:T(2,128)} %copy-done.34) | copy-start | bytes 6148
  542.1 45.4 %copy-start.44 = (f32[2,2,128]{2,1,0:T(2,128)S(1)}, f32[2,2,128]{2,1,0:T(2,128)}, u32[]{:S(2)}) copy-start(f32[2,2,128]{2,1,0:T(2,128)} %copy-done.43) | copy-start | bytes 6148
  542.1 46.0 %copy-start.40 = (s32[1024,1]{0,1:T(1,128)S(1)}, s32[1024,1]{0,1:T(1,128)}, u32[]{:S(2)}) copy-start(s32[1024,1]{0,1:T(1,128)} %copy-done.39) | copy-start | bytes 12292
  578.5 49.3 %all-to-all-start.3 = ((bf16[16,96,1024]{2,1,0:T(8,128)(2,1)}), bf16[16,96,1024]{2,1,0:T(8,128)(2,1)}, u32[]{:S(2)}, u32[]{:S(2)}) async-start(bf16[16,96,1024]{2,1,0:T(8,128)(2,1)} %bitcast.282), calls=%async_computation.3 | async-start | bytes 6291456 | tf_op jit(solution)/shard_map/all_to_all | solution.py:117
  587.2 103.2 %all-reduce.13.cloned.1.call-start = ((), (), s32[]{:S(2)}) async-start(), calls=%async_computation.15 | async-start | bytes 524288 | tf_op jit(solution)/shard_map/psum | solution.py:112
  593.4 9.3 copy-start.11
  602.7 13.9 copy-start.33
  642.3 48.2 %copy-start.2 = (bf16[128,1024]{1,0:T(8,128)(2,1)S(1)}, bf16[128,1024]{1,0:T(8,128)(2,1)}, u32[]{:S(2)}) copy-start(bf16[128,1024]{1,0:T(8,128)(2,1)} %all-reduce.11.cloned.1.call-done) | copy-start | bytes 786436
  642.3 48.2 %copy-start.31 = (f32[1024]{0:T(1024)S(1)}, f32[1024]{0:T(1024)}, u32[]{:S(2)}) copy-start(f32[1024]{0:T(1024)} %copy-done.30) | copy-start | bytes 12292
  642.3 48.1 %copy-start.49 = (f32[128]{0:T(128)S(1)}, f32[128]{0:T(128)}, u32[]{:S(2)}) copy-start(f32[128]{0:T(128)} %copy-done.48) | copy-start | bytes 1540
  642.3 49.5 %copy-start.9 = (bf16[128,1024]{1,0:T(8,128)(2,1)S(1)}, bf16[128,1024]{1,0:T(8,128)(2,1)}, u32[]{:S(2)}) copy-start(bf16[128,1024]{1,0:T(8,128)(2,1)} %param.27) | copy-start | bytes 786436
  642.3 49.5 %copy-start.52 = (f32[128]{0:T(128)S(1)}, f32[128]{0:T(128)}, u32[]{:S(2)}) copy-start(f32[128]{0:T(128)} %get-tuple-element.43) | copy-start | bytes 1540
  642.3 50.2 %copy-start.27 = (f32[2,64,2,128]{3,1,2,0:T(8,128)S(1)}, f32[2,64,2,128]{3,1,2,0:T(8,128)}, u32[]{:S(2)}) copy-start(f32[2,64,2,128]{3,1,2,0:T(8,128)} %get-tuple-element.48) | copy-start | bytes 393220
  646.4 120.0 %reduce-scatter.31.cloned.1.call-start = ((), (), s32[]{:S(2)}) async-start(), calls=%async_computation.24 | async-start | bytes 557056
  646.5 46.0 %copy-start.28 = (bf16[128,32]{0,1:T(8,128)(2,1)}, bf16[128,32]{0,1:T(8,128)(2,1)S(1)}, u32[]{:S(2)}) copy-start(bf16[128,32]{0,1:T(8,128)(2,1)S(1)} %multiply_convert_fusion.5) | copy-start | bytes 24580
  693.1 7.4 copy-start.50
  700.5 134.4 %reduce-scatter.33.cloned.1.call-start = ((), (), s32[]{:S(2)}) async-start(), calls=%async_computation.25 | async-start | bytes 557056 | tf_op jit(solution)/shard_map/reshape | solution.py:407
  706.5 147.4 %reduce-scatter.29.cloned.1.call-start = ((), (), s32[]{:S(2)}) async-start(), calls=%async_computation.23 | async-start | bytes 786432 | tf_op jit(solution)/shard_map/reduce_scatter | solution.py:338
  710.0 164.3 %reduce-scatter.27.cloned.1.call-start = ((), (), s32[]{:S(2)}) async-start(), calls=%async_computation.22 | async-start | bytes 786432 | tf_op jit(solution)/shard_map/reduce_scatter | solution.py:335
  714.2 180.6 %reduce-scatter.25.cloned.1.call-start = ((), (), s32[]{:S(2)}) async-start(), calls=%async_computation.21 | async-start | bytes 786432 | tf_op jit(solution)/shard_map/reduce_scatter | solution.py:332
  718.6 311.7 %reduce-scatter.23.cloned.1.call-start = ((), (), s32[]{:S(2)}) async-start(), calls=%async_computation.20 | async-start | bytes 270336 | tf_op jit(solution)/shard_map/reduce_scatter | solution.py:466
  719.7 441.3 %reduce-scatter.21.cloned.1.call-start = ((), (), s32[]{:S(2)}) async-start(), calls=%async_computation.19 | async-start | bytes 540672 | tf_op jit(solution)/shard_map/reduce_scatter | solution.py:457
  720.9 570.9 %reduce-scatter.15.cloned.1.call-start = ((), (), s32[]{:S(2)}) async-start(), calls=%async_computation.16 | async-start | bytes 540672 | tf_op jit(solution)/shard_map/reduce_scatter | solution.py:442
  724.5 609.8 %all-reduce.15.cloned.1.call-start = ((), (), s32[]{:S(2)}) async-start(), calls=%async_computation.26 | async-start | bytes 1048576 | tf_op jit(solution)/shard_map/psum | solution.py:112
  725.9 874.7 %copy-start.51 = (f32[128]{0:T(128)S(1)}, f32[128]{0:T(128)}, u32[]{:S(2)}) copy-start(f32[128]{0:T(128)} %get-tuple-element.41) | copy-start | bytes 1540
  836.8 632.0 %reduce-scatter.19.cloned.1.call-start = ((), (), s32[]{:S(2)}) async-start(), calls=%async_computation.18 | async-start | bytes 270336 | tf_op jit(solution)/shard_map/reduce_scatter | solution.py:451
  877.9 721.4 %reduce-scatter.17.cloned.1.call-start = ((), (), s32[]{:S(2)}) async-start(), calls=%async_computation.17 | async-start | bytes 270336 | tf_op jit(solution)/shard_map/reduce_scatter | solution.py:448
  (22 other events, 76.9 us)
Sparse Core Ops, SparseCore 0:
  307.0 40.7 all-reduce.10
  646.5 43.8 all-reduce.12
  700.6 65.8 reduce-scatter.30
  770.5 64.3 reduce-scatter.32
  837.6 16.1 reduce-scatter.28
  856.1 18.0 reduce-scatter.26
  876.6 18.1 reduce-scatter.24
  897.2 133.0 reduce-scatter.22
  1032.7 128.2 reduce-scatter.20
  1163.3 128.5 reduce-scatter.14
  1294.9 39.3 all-reduce.14
  1336.5 132.2 reduce-scatter.18
  1471.2 128.0 reduce-scatter.16
where the time goes:
time: 1620 us; the launch traced here: 1610 us
  waiting for transfers between devices  902 us (56%)
  blocking collectives  485 us (30%)
  other arithmetic  60 us (4%)
  local copies, waits for them, and re-layouts  59 us (4%)
  matrix products  56.2 us (3%)
  starting transfers between devices  30.9 us (2%)
  between operations  16.6 us (1%)
    unnamed x2, blocking collectives  134 us
    reduce_scatter x1, waiting for transfers between devices, per_device(): lax.psum_scatter(grads_router[back].astype(jnp.bfloat16), ('dp', 'context...  134 us
    reduce_scatter x1, waiting for transfers between devices, per_device(): lax.psum_scatter(grads_query[back].astype(jnp.bfloat16), ('dp', 'context'...  130 us
    reduce_scatter x1, waiting for transfers between devices, per_device(): lax.psum_scatter(grads_key[back].astype(jnp.bfloat16), ('dp', 'context'),...  129 us
    reduce_scatter x1, waiting for transfers between devices, per_device(): lax.psum_scatter(grads_out[back].astype(jnp.bfloat16), ('dp', 'context'),...  128 us
    psum x3, waiting for transfers between devices, over_tensor(): lax.psum(for_sending(parts), 'tensor')  107 us
    all_gather x1, blocking collectives, fetch_layer(): lax.all_gather(w_router[current], ('dp', 'context'), axis=0, tiled=True)  68.9 us
    reduce_scatter x1, waiting for transfers between devices, per_device(): lax.psum_scatter(grads_value[back].astype(jnp.bfloat16), ('dp', 'context'...  67.3 us
  transfers between devices with their start and end apart: 17, of which 15 were waited for; matrix products, arithmetic and copies ran while one was open for 7% of the time, Pallas kernels for 0%

commit v1 on v0

v1 whole, which is shorter than its diff:
```python
import functools
import math

import jax
import jax.numpy as jnp
from jax import lax
from jax.experimental import pallas as pl
from jax.experimental.pallas import tpu as pltpu
from jax.sharding import PartitionSpec as P

HEAD = 64
EPS = 1e-06
NEG = -1e30
F32 = jnp.float32
BF16 = jnp.bfloat16
TAIL = 128
VMEM_BYTES = 60 * 1024 * 1024


def dot(a, b):
    return jnp.dot(a, b, preferred_element_type=F32)


def dot_nt(a, b):
    return lax.dot_general(a, b, (((1,), (1,)), ((), ())), preferred_element_type=F32)


def dot_tn(a, b):
    return lax.dot_general(a, b, (((0,), (0,)), ((), ())), preferred_element_type=F32)


def remote(src, dst, send_sem, recv_sem, device):
    return pltpu.make_async_remote_copy(
        src_ref=src,
        dst_ref=dst,
        send_sem=send_sem,
        recv_sem=recv_sem,
        device_id=device,
        device_id_type=pl.DeviceIdType.MESH,
    )


def loop(start, stop, step):
    def body(k, carry):
        step(k)
        return carry

    lax.fori_loop(start, stop, body, 0)


class Gather:
    def __init__(self, count, me, core, peer, sibling, table, sems):
        self.count, self.me, self.core = count, me, core
        self.peer, self.sibling, self.table, self.sems = peer, sibling, table, sems

    def far(self, k):
        mine = self.table.at[self.me, self.core]
        return remote(mine, mine, self.sems.at[0, k], self.sems.at[1, k], self.peer(k))

    def near(self, k):
        chunk = self.table.at[lax.rem(self.me + self.count - k, self.count), self.core]
        return remote(chunk, chunk, self.sems.at[2, k], self.sems.at[3, k], self.sibling)

    def start(self):
        loop(1, self.count, lambda k: self.far(k).start())
        self.near(0).start()

    def forward(self):
        def step(k):
            self.far(k).wait_recv()
            self.near(k).start()

        loop(1, self.count, step)

    def finish(self):
        loop(0, self.count, lambda k: self.near(k).wait_recv())

    def drain(self):
        loop(1, self.count, lambda k: self.far(k).wait_send())
        loop(0, self.count, lambda k: self.near(k).wait_send())


class Scatter:
    def __init__(self, count, me, core, peer, sibling, parts, half, landed, sems):
        self.count, self.me, self.core = count, me, core
        self.peer, self.sibling = peer, sibling
        self.parts, self.half, self.landed, self.sems = parts, half, landed, sems

    def near(self):
        return remote(
            self.parts.at[:, 1 - self.core],
            self.half,
            self.sems.at[0, 0],
            self.sems.at[1, 0],
            self.sibling,
        )

    def far(self, k):
        there = lax.rem(self.me + k, self.count)
        return remote(
            self.half.at[there],
            self.landed.at[k],
            self.sems.at[0, k],
            self.sems.at[1, k],
            self.peer(k),
        )

    def start(self):
        self.near().start()

    def send(self):
        self.near().wait_recv()

        def add(there):
            mine = self.parts[there, self.core].astype(F32)
            self.half[there] = (mine + self.half[there].astype(F32)).astype(BF16)

        def step(k):
            add(lax.rem(self.me + k, self.count))
            self.far(k).start()

        loop(1, self.count, step)
        add(self.me)

    def total(self):
        def step(k, acc):
            self.far(k).wait_recv()
            return acc + self.landed[k].astype(F32)

        return lax.fori_loop(1, self.count, step, self.half[self.me].astype(F32))

    def drain(self):
        self.near().wait_send()
        loop(1, self.count, lambda k: self.far(k).wait_send())


def layer(
    sizes,
    xin,
    cot,
    segc,
    rts,
    wpk,
    wgi,
    wui,
    wdi,
    o_h,
    o_ig,
    o_w,
    o_t,
    o_wg,
    o_wu,
    o_wd,
    wall,
    cotall,
    ball,
    kv,
    wg,
    wu,
    wd,
    a_ref,
    qs,
    p_ref,
    ds_ref,
    o_ref,
    part,
    ybuf,
    hall,
    dall,
    igall,
    dgp_ref,
    dup_ref,
    ug_ref,
    dbs,
    dbs_half,
    dbs_land,
    ys,
    ys_half,
    ys_land,
    gg,
    gu,
    gd,
    gg_land,
    gu_land,
    gd_land,
    dos,
    dq_ref,
    dkv,
    dkv_half,
    dkv_land,
    wgs,
    wgs_half,
    wgs_land,
    tail_y,
    s_wall,
    s_cot,
    s_ball,
    s_kv,
    s_exp,
    s_y1,
    s_dbs,
    s_ys,
    s_grad,
    s_dall,
    s_dkv,
    s_y2,
    s_wgs,
    s_fin,
):
    n_dp, n_ctx, n_ten = sizes
    nj = n_ctx // 2
    nq = n_dp * nj
    rows, width = xin.shape
    seq = n_ctx * rows
    quarter = rows // n_ten
    d, c, r = lax.axis_index("dp"), lax.axis_index("context"), lax.axis_index("tensor")
    core, j = lax.rem(c, 2), c // 2
    q = d * nj + j

    def at(dp, context, tensor):
        return {"dp": dp, "context": context, "tensor": tensor}

    def plane(k):
        there = lax.rem(q + k, nq)
        return at(there // nj, lax.rem(there, nj) * 2 + core, r)

    def along(k):
        return at(d, lax.rem(j + k, nj) * 2 + core, r)

    def tensor(k):
        return at(d, c, lax.rem(r + k, n_ten))

    def holder(o):
        return at(lax.rem(d + o // n_ten, n_dp), c, lax.rem(r + lax.rem(o, n_ten), n_ten))

    sibling = at(d, c + 1 - 2 * core, r)

    barrier = pltpu.get_barrier_semaphore()

    def greet(device):
        pl.semaphore_signal(barrier, inc=1, device_id=device, device_id_type=pl.DeviceIdType.MESH)

    loop(1, nq, lambda k: greet(plane(k)))
    greet(sibling)
    loop(1, n_dp * n_ten, lambda o: greet(holder(o)))
    pl.semaphore_wait(barrier, nq + n_dp * n_ten - 1)

    wide = pl.ds(pl.multiple_of(r * quarter, quarter), quarter)

    g_wall = Gather(nq, q, core, plane, sibling, wall, s_wall)
    wall[q, core] = wpk[...]
    g_wall.start()

    half_d, cut = wgi.shape[1], wgi.shape[2]

    def d_rows(dp):
        return pl.ds(pl.multiple_of(dp * half_d, half_d), half_d)

    def f_rows(ten):
        return pl.ds(pl.multiple_of(ten * cut, cut), cut)

    def expert_copies(o):
        there = lax.rem(d + o // n_ten, n_dp)
        place = wg.at[d_rows(d), f_rows(r)]
        place_u = wu.at[d_rows(d), f_rows(r)]
        place_d = wd.at[f_rows(r), d_rows(d)]
        return (
            remote(wgi.at[there], place, s_exp.at[0, o], s_exp.at[1, o], holder(o)),
            remote(wui.at[there], place_u, s_exp.at[2, o], s_exp.at[3, o], holder(o)),
            remote(wdi.at[there], place_d, s_exp.at[4, o], s_exp.at[5, o], holder(o)),
        )

    def start_experts(o):
        for copy in expert_copies(o):
            copy.start()

    x = xin[...].astype(F32)
    inv = lax.rsqrt(jnp.mean(x * x, axis=-1, keepdims=True) + EPS)
    lane = lax.broadcasted_iota(jnp.int32, (1, 128), 1)
    low_half = lax.rem(lane, HEAD) < HEAD // 2
    group_of = lane // HEAD
    rate = jnp.exp(
        lax.rem(lane, HEAD // 2).astype(F32) * (-2.0 * math.log(10000.0) / HEAD)
    )
    row_index = c * rows + lax.broadcasted_iota(jnp.int32, (rows, 1), 0)
    angle = row_index.astype(F32) * rate
    cosine = jnp.cos(angle)
    sine = jnp.where(low_half, -1.0, 1.0) * jnp.sin(angle)

    def partner(z):
        return jnp.where(
            low_half, pltpu.roll(z, 128 - HEAD // 2, 1), pltpu.roll(z, HEAD // 2, 1)
        )

    def rope(z):
        return z * cosine + partner(z) * sine

    def unrope(z):
        return z * cosine - partner(z) * sine

    wg[d_rows(d), f_rows(r)] = wgi[d]
    wu[d_rows(d), f_rows(r)] = wui[d]
    wd[f_rows(r), d_rows(d)] = wdi[d]
    g_cot = Gather(nq, q, core, plane, sibling, cotall, s_cot)
    cotall[q, core] = cot[wide]

    g_wall.forward()
    g_wall.finish()
    loop(1, n_dp * n_ten, start_experts)
    g_cot.start()

    tails = wall[:, :, :, 768:896].reshape(width, TAIL)
    gains = tails.astype(F32).T
    attn_gain, ffn_gain = gains[32:33], gains[33:34]
    a_ref[...] = (x * inv * attn_gain).astype(BF16)

    qkv = dot(a_ref[...], wall[:, :, :, 0:512].reshape(width, 512))
    for t in range(2):
        turned = rope(qkv[:, 128 * t : 128 * t + 128]) * 0.125
        for g in range(2):
            qs[2 * t + g] = jnp.where(group_of == g, turned, 0.0).astype(BF16)
    kv[j, core, :, 0:128] = rope(qkv[:, 256:384]).astype(BF16)
    kv[j, core, :, 128:256] = qkv[:, 384:512].astype(BF16)
    g_kv = Gather(nj, j, core, along, sibling, kv, s_kv)
    g_kv.start()

    numbers = wall[pl.ds(d * nj, nj), :, :, 768:896].reshape(nj * 64, TAIL).astype(F32)
    held = jnp.where((lane >= 34) & (lane < 38), numbers, 1e9)
    mine = segc[...]
    first = jnp.zeros((rows, 1), F32)
    for s in range(1, 4):
        below = jnp.sum(jnp.where(held < s - 0.5, 1.0, 0.0), axis=0, keepdims=True)
        below = jnp.sum(below, axis=1, keepdims=True)
        first = jnp.where(mine == s, below, first)
    first = first.astype(jnp.int32)
    columns = lax.broadcasted_iota(jnp.int32, (rows, seq), 1)
    allowed = (columns >= first) & (columns <= row_index)

    g_kv.forward()
    g_kv.finish()

    o_ref[...] = jnp.zeros_like(o_ref)

    def head_forward(i):
        scores = dot_nt(qs[i], kv[:, :, :, 0:128].reshape(seq, 128))
        scores = jnp.where(allowed, scores, NEG)
        top = jnp.max(scores, axis=-1, keepdims=True)
        expo = jnp.where(allowed, jnp.exp(scores - top), 0.0)
        weights = (expo * (1.0 / jnp.sum(expo, axis=-1, keepdims=True))).astype(BF16)
        p_ref[i] = weights
        out = dot(weights, kv[:, :, :, 128:256].reshape(seq, 128))
        o_ref[i // 2] += jnp.where(group_of == lax.rem(i, 2), out, 0.0)

    loop(0, 4, head_forward)
    o_low = jnp.concatenate([o_ref[0], o_ref[1]], axis=1).astype(BF16)
    w_out = wall[:, :, :, 512:768].reshape(width, 256)
    part[0] = dot_nt(o_low, w_out).astype(BF16).reshape(n_ten, quarter, width)

    def tensor_copy(which, sems, k):
        return remote(
            part.at[which, lax.rem(r + k, n_ten)],
            ybuf.at[which, k],
            sems.at[0, k],
            sems.at[1, k],
            tensor(k),
        )

    loop(1, n_ten, lambda k: tensor_copy(0, s_y1, k).start())
    g_cot.forward()
    hidden = xin[wide].astype(F32) + part[0, r].astype(F32)
    for k in range(1, n_ten):
        tensor_copy(0, s_y1, k).wait_recv()
        hidden = hidden + ybuf[0, k].astype(F32)

    inv_two = lax.rsqrt(jnp.mean(hidden * hidden, axis=-1, keepdims=True) + EPS)
    b_own = (hidden * inv_two * ffn_gain).astype(BF16)
    logits = jnp.where(lane < 32, dot(b_own, tails), NEG)
    expo = jnp.exp(logits - jnp.max(logits, axis=-1, keepdims=True))
    probs = expo / jnp.sum(expo, axis=-1, keepdims=True)
    routed = jnp.zeros((quarter, 128), F32)
    routes = rts[wide]
    for k in range(routes.shape[1]):
        routed = routed + jnp.where(routes[:, k : k + 1] == lane, 1.0, 0.0)
    gates = probs * routed
    gates_high = gates.astype(BF16).astype(F32)
    ball[q, core, :, 0:width] = b_own
    ball[q, core, :, width : width + TAIL] = (
        gates_high + pltpu.roll(gates - gates_high, 32, 1)
    ).astype(BF16)
    g_ball = Gather(nq, q, core, plane, sibling, ball, s_ball)
    g_ball.start()
    g_ball.forward()
    g_cot.finish()

    def wait_experts(o):
        for copy in expert_copies(o):
            copy.wait_recv()

    loop(1, n_dp * n_ten, wait_experts)
    g_ball.finish()

    expert = 2 * c + d
    gate_lane = (lane == expert) | (lane == expert + 32)
    block = 8 * quarter
    steps = nq // 4

    def tokens(ref, i, cut_at, cut_to):
        return ref[pl.ds(4 * i, 4), :, :, cut_at:cut_to].reshape(block, cut_to - cut_at)

    def rows_of(i):
        return pl.ds(pl.multiple_of(i * block, block), block)

    def expert_block(i):
        b = tokens(ball, i, 0, width)
        packed = tokens(ball, i, width, width + TAIL).astype(F32)
        gate = jnp.sum(jnp.where(gate_lane, packed, 0.0), axis=-1, keepdims=True)
        gp = dot(b, wg[...])
        up = dot(b, wu[...])
        du = dot_nt(tokens(cotall, i, 0, width), wd[...])
        sigma = 1.0 / (1.0 + jnp.exp(-gp))
        silu = gp * sigma
        u = (silu * up).astype(BF16).astype(F32)
        dgate = jnp.sum(du * u, axis=-1, keepdims=True)
        du = gate * du
        dgp = (du * up * sigma * (1.0 + gp * (1.0 - sigma))).astype(BF16)
        dup = (du * silu).astype(BF16)
        dgp_ref[rows_of(i)] = dgp
        dup_ref[rows_of(i)] = dup
        ug_ref[rows_of(i)] = (gate * u).astype(BF16)
        db = dot_nt(dgp, wg[...]) + dot_nt(dup, wu[...])
        dbs[pl.ds(4 * i, 4), :, :, 0:width] = db.astype(BF16).reshape(4, 2, quarter, width)
        dbs[pl.ds(4 * i, 4), :, :, width : width + TAIL] = (
            jnp.where(lane == expert, dgate, 0.0).astype(BF16).reshape(4, 2, quarter, TAIL)
        )

    loop(0, steps, expert_block)
    x_dbs = Scatter(nq, q, core, plane, sibling, dbs, dbs_half, dbs_land, s_dbs)
    x_dbs.start()

    def down_block(i):
        y = dot(ug_ref[rows_of(i)], wd[...])
        ys[pl.ds(4 * i, 4)] = y.astype(BF16).reshape(4, 2, quarter, width)

    loop(0, steps, down_block)
    x_dbs.send()
    x_ys = Scatter(nq, q, core, plane, sibling, ys, ys_half, ys_land, s_ys)
    x_ys.start()

    all_cot = cotall[...].reshape(nq * 2 * quarter, width)
    all_b = ball[:, :, :, 0:width].reshape(nq * 2 * quarter, width)
    gd[...] = dot_tn(ug_ref[...], all_cot).astype(BF16)
    gg[...] = dot_tn(all_b, dgp_ref[...]).astype(BF16)
    gu[...] = dot_tn(all_b, dup_ref[...]).astype(BF16)

    def grad_copies(o):
        dp, ten = lax.rem(d + o // n_ten, n_dp), lax.rem(r + lax.rem(o, n_ten), n_ten)
        return (
            remote(
                gg.at[d_rows(dp), f_rows(ten)], gg_land.at[o], s_grad.at[0, o], s_grad.at[1, o],
                holder(o),
            ),
            remote(
                gu.at[d_rows(dp), f_rows(ten)], gu_land.at[o], s_grad.at[2, o], s_grad.at[3, o],
                holder(o),
            ),
            remote(
                gd.at[f_rows(ten), d_rows(dp)], gd_land.at[o], s_grad.at[4, o], s_grad.at[5, o],
                holder(o),
            ),
        )

    def start_grads(o):
        for copy in grad_copies(o):
            copy.start()

    summed = x_dbs.total()
    x_ys.send()
    dprobs = routed * summed[:, width : width + TAIL]
    dlogits = probs * (dprobs - jnp.sum(probs * dprobs, axis=-1, keepdims=True))
    dlogits = jnp.where(lane < 32, dlogits, 0.0).astype(BF16)
    db = summed[:, 0:width] + dot_nt(dlogits, tails)
    w_db = db * ffn_gain
    grad_hidden = (
        cot[wide].astype(F32)
        + inv_two * w_db
        - hidden * inv_two**3 * (jnp.sum(w_db * hidden, axis=-1, keepdims=True) / width)
    )
    ffn_gain_rows = (db * hidden * inv_two).astype(BF16)
    dall[r] = grad_hidden.astype(BF16)

    def spread(table, sems, k):
        mine = table.at[r]
        return remote(mine, mine, sems.at[0, k], sems.at[1, k], tensor(k))

    loop(1, n_ten, lambda k: spread(dall, s_dall, k).start())
    one_hot = lax.broadcasted_iota(jnp.int32, (rows, TAIL), 1)
    ones_ffn = jnp.where(one_hot[0:quarter] == 32, 1.0, 0.0).astype(BF16)
    ones_attn = jnp.where(one_hot == 33, 1.0, 0.0).astype(BF16)
    tail_grad = dot_tn(b_own, dlogits) + dot_tn(ffn_gain_rows, ones_ffn)
    loop(1, n_ten, lambda k: spread(dall, s_dall, k).wait_recv())

    d_attn = dall[...].reshape(rows, width)
    do = dot(d_attn, w_out).astype(BF16)
    loop(1, n_dp * n_ten, start_grads)
    for t in range(2):
        tile = do[:, 128 * t : 128 * t + 128].astype(F32)
        for g in range(2):
            dos[2 * t + g] = jnp.where(group_of == g, tile, 0.0).astype(BF16)

    dq_ref[...] = jnp.zeros_like(dq_ref)

    def head_backward(i):
        go = dos[i]
        delta = jnp.sum(go.astype(F32) * o_ref[i // 2], axis=-1, keepdims=True)
        dp = dot_nt(go, kv[:, :, :, 128:256].reshape(seq, 128))
        grad = (p_ref[i].astype(F32) * (dp - delta)).astype(BF16)
        ds_ref[i] = grad
        dq = dot(grad, kv[:, :, :, 0:128].reshape(seq, 128))
        dq_ref[i // 2] += jnp.where(group_of == lax.rem(i, 2), dq, 0.0)

    loop(0, 4, head_backward)
    all_q = qs[...].reshape(4 * rows, 128)
    all_do = dos[...].reshape(4 * rows, 128)
    for i in range(4):
        span = slice(i * (seq // 4), (i + 1) * (seq // 4))
        place = slice(i * (nj // 4), (i + 1) * (nj // 4))
        dk = dot_tn(ds_ref[:, :, span].reshape(4 * rows, seq // 4), all_q)
        dv = dot_tn(p_ref[:, :, span].reshape(4 * rows, seq // 4), all_do)
        dkv[place, :, :, 0:128] = dk.astype(BF16).reshape(nj // 4, 2, rows, 128)
        dkv[place, :, :, 128:256] = dv.astype(BF16).reshape(nj // 4, 2, rows, 128)
    x_dkv = Scatter(nj, j, core, along, sibling, dkv, dkv_half, dkv_land, s_dkv)
    x_dkv.start()

    def to_rows(grad):
        return grad.astype(BF16).reshape(nq, 2, 32, grad.shape[1])

    a_low = a_ref[...]
    wgs[:, :, :, 512:768] = to_rows(dot_tn(d_attn, o_low))
    x_dkv.send()
    dq_lin = jnp.concatenate([unrope(dq_ref[0]), unrope(dq_ref[1])], axis=1) * 0.125
    dq_lin = dq_lin.astype(BF16)
    wgs[:, :, :, 0:256] = to_rows(dot_tn(a_low, dq_lin))
    da = dot_nt(dq_lin, wall[:, :, :, 0:256].reshape(width, 256))
    grad_kv = x_dkv.total()
    dkv_lin = jnp.concatenate([unrope(grad_kv[:, 0:128]), grad_kv[:, 128:256]], axis=1)
    dkv_lin = dkv_lin.astype(BF16)
    da = da + dot_nt(dkv_lin, wall[:, :, :, 256:512].reshape(width, 256))
    part[1] = da.astype(BF16).reshape(n_ten, quarter, width)
    loop(1, n_ten, lambda k: tensor_copy(1, s_y2, k).start())
    wgs[:, :, :, 256:512] = to_rows(dot_tn(a_low, dkv_lin))
    attn_gain_rows = (da * xin[...].astype(F32) * inv).astype(BF16)
    wgs[:, :, :, 768:896] = to_rows(tail_grad + dot_tn(attn_gain_rows, ones_attn))
    x_wgs = Scatter(nq, q, core, plane, sibling, wgs, wgs_half, wgs_land, s_wgs)
    x_wgs.start()

    hall[r] = (hidden + x_ys.total()).astype(BF16)
    loop(1, n_ten, lambda k: spread(hall, s_fin, k).start())

    grad_a = part[1, r].astype(F32)
    for k in range(1, n_ten):
        tensor_copy(1, s_y2, k).wait_recv()
        grad_a = grad_a + ybuf[1, k].astype(F32)
    x_own = xin[wide].astype(F32)
    inv_own = lax.rsqrt(jnp.mean(x_own * x_own, axis=-1, keepdims=True) + EPS)
    w_da = grad_a * attn_gain
    grad_x = (
        grad_hidden
        + inv_own * w_da
        - x_own * inv_own**3 * (jnp.sum(w_da * x_own, axis=-1, keepdims=True) / width)
    )
    igall[r] = grad_x.astype(BF16)

    def spread_ig(k):
        mine = igall.at[r]
        return remote(mine, mine, s_fin.at[2, k], s_fin.at[3, k], tensor(k))

    loop(1, n_ten, lambda k: spread_ig(k).start())
    x_wgs.send()

    def wait_grads(o):
        for copy in grad_copies(o):
            copy.wait_recv()

    loop(1, n_dp * n_ten, wait_grads)

    def reduce_grads(out, land, own):
        same = own
        for k in range(1, n_ten):
            same = same + land[k].astype(F32)
        out[d] = same
        other = land[n_ten].astype(F32)
        for k in range(1, n_ten):
            other = other + land[n_ten + k].astype(F32)
        out[1 - d] = other

    reduce_grads(o_wg, gg_land, gg[d_rows(d), f_rows(r)].astype(F32))
    reduce_grads(o_wu, gu_land, gu[d_rows(d), f_rows(r)].astype(F32))
    reduce_grads(o_wd, gd_land, gd[f_rows(r), d_rows(d)].astype(F32))

    loop(1, n_ten, lambda k: spread(hall, s_fin, k).wait_recv())
    o_h[...] = hall[...]
    loop(1, n_ten, lambda k: spread_ig(k).wait_recv())
    o_ig[...] = igall[...].astype(F32)

    grads = x_wgs.total()
    o_w[...] = grads[:, 0:768]
    tail_y[0] = grads[:, 768:896]

    def tail_copy(k):
        return remote(tail_y.at[0], tail_y.at[k], s_fin.at[4, k], s_fin.at[5, k], tensor(k))

    loop(1, n_ten, lambda k: tail_copy(k).start())
    tail_sum = grads[:, 768:896]
    for k in range(1, n_ten):
        tail_copy(k).wait_recv()
        tail_sum = tail_sum + tail_y[k]
    o_t[...] = tail_sum

    for gather in (g_wall, g_cot, g_kv, g_ball):
        gather.drain()
    for scatter in (x_dbs, x_ys, x_dkv, x_wgs):
        scatter.drain()

    def drain_tensor(k):
        tensor_copy(0, s_y1, k).wait_send()
        tensor_copy(1, s_y2, k).wait_send()
        spread(dall, s_dall, k).wait_send()
        spread(hall, s_fin, k).wait_send()
        spread_ig(k).wait_send()
        tail_copy(k).wait_send()

    loop(1, n_ten, drain_tensor)

    def drain_experts(o):
        for copy in expert_copies(o) + grad_copies(o):
            copy.wait_send()

    loop(1, n_dp * n_ten, drain_experts)


def call_layer(sizes, xin, cot, segc, rts, wpk, wgi, wui, wdi):
    n_dp, n_ctx, n_ten = sizes
    nj = n_ctx // 2
    nq = n_dp * nj
    rows, width = xin.shape
    seq = n_ctx * rows
    quarter = rows // n_ten
    half_d, cut = wgi.shape[1], wgi.shape[2]
    hidden_units = cut * n_ten
    packed = wpk.shape[1]
    all_rows = nq * 2 * quarter
    holders = n_dp * n_ten

    def shape(*dims, kind=F32):
        return jax.ShapeDtypeStruct(dims, kind)

    def low(*dims):
        return pltpu.VMEM(dims, BF16)

    def full(*dims):
        return pltpu.VMEM(dims, F32)

    def sems(*dims):
        return pltpu.SemaphoreType.DMA(dims)

    scratch = [
        low(nq, 2, 32, packed),
        low(nq, 2, quarter, width),
        low(nq, 2, quarter, width + TAIL),
        low(nj, 2, rows, 256),
        low(width, hidden_units),
        low(width, hidden_units),
        low(hidden_units, width),
        low(rows, width),
        low(4, rows, 128),
        low(4, rows, seq),
        low(4, rows, seq),
        full(2, rows, 128),
        low(2, n_ten, quarter, width),
        low(2, n_ten, quarter, width),
        low(n_ten, quarter, width),
        low(n_ten, quarter, width),
        low(n_ten, quarter, width),
        low(all_rows, hidden_units),
        low(all_rows, hidden_units),
        low(all_rows, hidden_units),
        low(nq, 2, quarter, width + TAIL),
        low(nq, quarter, width + TAIL),
        low(nq, quarter, width + TAIL),
        low(nq, 2, quarter, width),
        low(nq, quarter, width),
        low(nq, quarter, width),
        low(width, hidden_units),
        low(width, hidden_units),
        low(hidden_units, width),
        low(holders, half_d, cut),
        low(holders, half_d, cut),
        low(holders, cut, half_d),
        low(4, rows, 128),
        full(2, rows, 128),
        low(nj, 2, rows, 256),
        low(nj, rows, 256),
        low(nj, rows, 256),
        low(nq, 2, 32, packed),
        low(nq, 32, packed),
        low(nq, 32, packed),
        full(n_ten, 32, TAIL),
        sems(4, nq),
        sems(4, nq),
        sems(4, nq),
        sems(4, nj),
        sems(6, holders),
        sems(2, n_ten),
        sems(2, nq),
        sems(2, nq),
        sems(6, holders),
        sems(2, n_ten),
        sems(2, nj),
        sems(2, n_ten),
        sems(2, nq),
        sems(6, n_ten),
    ]
    flops = 2 * (9 * all_rows * width * hidden_units + 4 * rows * width * 768)
    return pl.pallas_call(
        functools.partial(layer, sizes),
        out_shape=(
            shape(n_ten, quarter, width, kind=BF16),
            shape(n_ten, quarter, width),
            shape(32, 768),
            shape(32, TAIL),
            shape(2, half_d, cut),
            shape(2, half_d, cut),
            shape(2, cut, half_d),
        ),
        in_specs=[pl.BlockSpec(memory_space=pltpu.VMEM)] * 8,
        out_specs=[pl.BlockSpec(memory_space=pltpu.VMEM)] * 7,
        scratch_shapes=scratch,
        compiler_params=pltpu.CompilerParams(
            collective_id=0, has_side_effects=True, vmem_limit_bytes=VMEM_BYTES
        ),
        cost_estimate=pl.CostEstimate(flops=flops, bytes_accessed=8 << 20, transcendentals=0),
    )(xin, cot, segc, rts, wpk, wgi, wui, wdi)


def swap_heads(table):
    a, b, c, d = [table[:, HEAD * i : HEAD * i + HEAD] for i in range(4)]
    return jnp.concatenate([a, c, b, d], axis=1)


def per_device(
    hidden_in,
    segments,
    routes,
    norm_attn,
    w_query,
    w_key,
    w_value,
    w_out,
    norm_ffn,
    w_router,
    w_gate,
    w_up,
    w_down,
    cotangent,
):
    sizes = (lax.axis_size("dp"), lax.axis_size("context"), lax.axis_size("tensor"))
    rows = hidden_in.shape[0]
    per_row = rows // 32
    packed = jnp.concatenate(
        [
            swap_heads(w_query[0]),
            w_key[0],
            w_value[0],
            swap_heads(w_out[0].T),
            w_router[0],
            norm_attn[0][:, None],
            norm_ffn[0][:, None],
            segments[0].reshape(32, per_row).astype(BF16),
            jnp.zeros((32, TAIL - 34 - per_row), BF16),
        ],
        axis=1,
    )
    out, grad, w_grads, tail, gate_grad, up_grad, down_grad = call_layer(
        sizes,
        hidden_in,
        cotangent,
        segments[0][:, None],
        routes[0],
        packed,
        w_gate[0],
        w_up[0],
        w_down[0],
    )
    return (
        out.reshape(hidden_in.shape),
        grad.reshape(hidden_in.shape),
        tail[:, 33][None],
        swap_heads(w_grads[:, 0:256])[None],
        w_grads[:, 256:384][None],
        w_grads[:, 384:512][None],
        swap_heads(w_grads[:, 512:768]).T[None],
        tail[:, 32][None],
        tail[:, 0:32][None],
        gate_grad[None],
        up_grad[None],
        down_grad[None],
    )


def solution(mesh):
    in_specs = (
        P(("dp", "context"), None),
        P("dp", "context"),
        P(None, ("dp", "context"), None),
        P(None, ("dp", "context")),
        P(None, ("dp", "context"), "tensor"),
        P(None, ("dp", "context"), "tensor"),
        P(None, ("dp", "context"), "tensor"),
        P(None, "tensor", ("dp", "context")),
        P(None, ("dp", "context")),
        P(None, ("dp", "context"), None),
        P(None, "context", "dp", "tensor"),
        P(None, "context", "dp", "tensor"),
        P(None, "context", "tensor", "dp"),
        P(("dp", "context"), None),
    )
    out_specs = (
        P(("dp", "context"), None),
        P(("dp", "context"), None),
        P(None, ("dp", "context")),
        P(None, ("dp", "context"), "tensor"),
        P(None, ("dp", "context"), "tensor"),
        P(None, ("dp", "context"), "tensor"),
        P(None, "tensor", ("dp", "context")),
        P(None, ("dp", "context")),
        P(None, ("dp", "context"), None),
        P(None, "context", "dp", "tensor"),
        P(None, "context", "dp", "tensor"),
        P(None, "context", "tensor", "dp"),
    )
    return jax.shard_map(
        per_device, mesh=mesh, in_specs=in_specs, out_specs=out_specs, check_vma=False
    )
```

time: 1620 us -> 228 us (0.14)
  waiting for transfers between devices: 902 us -> 0 us
  blocking collectives: 485 us -> 0 us
  Pallas kernels: 0 us -> 210 us
  other arithmetic: 60 us -> 1.42 us
  matrix products: 56.2 us -> 0 us
  local copies, waits for them, and re-layouts: 59 us -> 15.1 us
  starting transfers between devices: 30.9 us -> 0 us
    reduce_scatter x8 -> x0, waiting for transfers between devices: 641 us -> none  [the longest x1 134 us: per_device(): lax.psum_scatter(grads_router[back].astype(jnp.bfloat16), ('dp', 'context...]
    all_gather x11 -> x0, blocking collectives: 341 us -> none  [the longest x1 68.9 us: fetch_layer(): lax.all_gather(w_router[current], ('dp', 'context'), axis=0, tiled=True)]
    pallas_call x0 -> x1, Pallas kernels: none -> 210 us  [call_layer(): pl.pallas_call(functools.partial(layer, sizes), out_shape=(shape(n_ten, q...]
    unnamed x2 -> x0, blocking collectives: 134 us -> none
    psum x3 -> x0, waiting for transfers between devices: 107 us -> none  [over_tensor(): lax.psum(for_sending(parts), 'tensor')]
    reshape x1 -> x0, waiting for transfers between devices: 66.3 us -> none  [per_device(): grad_values.astype(jnp.bfloat16).reshape(rows_here, kv_here * HEAD)]
    dot_general x30 -> x0, matrix products: 56.2 us -> none  [the longest x1 4.44 us: experts_backward(): jnp.einsum('secd,efd->secf', upstream, down_map, preferred_element_type=j...]
    all_to_all x4 -> x0, waiting for transfers between devices: 47.5 us -> none  [route_rows(): lax.all_to_all(buffer, 'context', split_axis=0, concat_axis=0, tiled=True)]
  transfers between devices with their start and end apart: 17 -> 0, of which waited for: 15 -> 0; matrix products, arithmetic and copies ran while one was open for 7% -> 0% of each run, Pallas kernels for 0% -> 0%
where the time goes in v1:
time: 228 us
  Pallas kernels  210 us (92%)
  local copies, waits for them, and re-layouts  15.1 us (7%)
    pallas_call x1, Pallas kernels, call_layer(): pl.pallas_call(functools.partial(layer, sizes), out_shape=(shape(n_ten, q...  210 us
    unnamed x36, local copies, waits for them, and re-layouts  8.96 us

profile of v1, /device:TPU:0, one launch (start us, length us, event | category | flops | bytes accessed | tf_op | source)
XLA Modules:
  0.0 227.5 jit_solution(83705338257558826)
XLA Ops:
  0.6 0.0 copy-start.12
  0.7 0.6 copy-done.12
  1.3 0.0 copy-start.13
  1.3 0.1 convert_element_type.7
  1.4 0.5 copy-done.13
  2.0 0.0 copy-start.14
  2.0 0.1 copy.31
  2.1 0.6 copy-done.14
  2.6 0.0 copy-start.11
  2.6 0.1 copy.32
  2.7 0.6 copy-done.11
  3.3 0.7 copy.30
  4.0 0.0 copy-start.6
  4.0 0.0 copy-start.7
  4.1 0.7 copy.33.segc
  4.8 0.0 copy-done.6
  4.8 0.0 copy-done.7
  4.8 0.0 copy-start.10
  4.8 0.1 fusion.1
  4.9 0.0 copy-start.8
  4.9 0.0 copy-start.9
  4.9 0.6 copy-done.10
  5.5 0.1 copy-done.8
  5.6 0.0 copy-done.9
  5.6 0.7 concatenate.9.wpk
  6.3 210.3 %shard_map.229 = (bf16[4,32,1024]{2,1,0:T(8,128)(2,1)}, f32[4,32,1024]{2,1,0:T(8,128)}, f32[32,768]{1,0:T(8,128)}, f32[32,128]{1,0:T(8,128)}, f32[2,512,128]{2,1...) custom-call(bf16[128,1024]{1,0:T(8,128)(2,1)} %xin.1, bf16[128,1024]{1,0:T(8,128)(2,1)} %cot.1, ...), custom_call_target="tpu_custom_call" | custom-call | flops 10468982784 | bytes 8388608 | tf_op jit(solution)/shard_map/pallas_call | solution.py:724
  216.6 0.0 copy-start.4
  216.6 1.5 slice_reduce_fusion
  218.1 1.3 slice_bitcast_fusion
  219.4 0.0 copy-start.5
  219.4 0.0 copy-start.3
  219.4 1.4 slice_bitcast_fusion.1
  220.8 0.0 copy-done.4
  220.8 0.1 fusion
  220.9 0.7 maximum_bitcast_fusion.1
  221.6 0.7 maximum_bitcast_fusion
  222.3 0.0 copy-done.5
  222.3 0.7 copy.39
  223.0 0.0 copy-done.3
  223.0 0.0 copy-start.2
  223.0 0.8 copy.40
  223.8 0.4 copy-done.2
  224.3 0.0 copy-start.1
  224.3 0.8 copy.41
  225.1 0.4 copy-done.1
  225.5 0.8 copy.42
  226.3 0.4 copy-done
  226.7 0.8 copy.43
  (3 shorter events, 0.0 us)
Async XLA Ops:
  0.6 0.7 copy-start.12
  1.3 0.7 copy-start.13
  2.0 0.7 copy-start.14
  2.6 0.7 copy-start.11
  4.0 0.7 copy-start.6
  4.0 0.7 copy-start.7
  4.8 0.7 copy-start.10
  4.9 0.7 copy-start.8
  4.9 0.7 copy-start.9
  216.6 4.3 %copy-start.4 = (f32[32,768]{1,0:T(8,128)S(1)}, f32[32,768]{1,0:T(8,128)}, u32[]{:S(2)}) copy-start(f32[32,768]{1,0:T(8,128)} %get-tuple-element.22) | copy-start | bytes 294916
  219.4 2.9 %copy-start.5 = (bf16[4,32,1024]{2,1,0:T(8,128)(2,1)S(1)}, bf16[4,32,1024]{2,1,0:T(8,128)(2,1)}, u32[]{:S(2)}) copy-start(bf16[4,32,1024]{2,1,0:T(8,128)(2,1)} %get-tuple-element.19) | copy-start | bytes 786436
  219.4 3.6 %copy-start.3 = (f32[4,32,1024]{2,1,0:T(8,128)S(1)}, f32[4,32,1024]{2,1,0:T(8,128)}, u32[]{:S(2)}) copy-start(f32[4,32,1024]{2,1,0:T(8,128)} %get-tuple-element.20) | copy-start | bytes 1572868
  223.0 1.2 copy-start.2
  224.3 1.2 copy-start.1
  225.5 1.2 copy-start

commit v2 on v1

--- a/solution.py
+++ b/solution.py
@@ -183,6 +183,9 @@
     gg_land,
     gu_land,
     gd_land,
+    gg_out,
+    gu_out,
+    gd_out,
     dos,
     dq_ref,
     dkv,
@@ -230,9 +233,7 @@
     def tensor(k):
         return at(d, c, lax.rem(r + k, n_ten))
 
-    def holder(o):
-        return at(lax.rem(d + o // n_ten, n_dp), c, lax.rem(r + lax.rem(o, n_ten), n_ten))
-
+    partner_dp = at(1 - d, c, r)
     sibling = at(d, c + 1 - 2 * core, r)
 
     barrier = pltpu.get_barrier_semaphore()
@@ -242,8 +243,8 @@
 
     loop(1, nq, lambda k: greet(plane(k)))
     greet(sibling)
-    loop(1, n_dp * n_ten, lambda o: greet(holder(o)))
-    pl.semaphore_wait(barrier, nq + n_dp * n_ten - 1)
+    loop(1, n_ten, lambda k: greet(tensor(k)))
+    pl.semaphore_wait(barrier, nq + n_ten - 1)
 
     wide = pl.ds(pl.multiple_of(r * quarter, quarter), quarter)
 
@@ -259,20 +260,40 @@
     def f_rows(ten):
         return pl.ds(pl.multiple_of(ten * cut, cut), cut)
 
-    def expert_copies(o):
-        there = lax.rem(d + o // n_ten, n_dp)
-        place = wg.at[d_rows(d), f_rows(r)]
-        place_u = wu.at[d_rows(d), f_rows(r)]
-        place_d = wd.at[f_rows(r), d_rows(d)]
-        return (
-            remote(wgi.at[there], place, s_exp.at[0, o], s_exp.at[1, o], holder(o)),
-            remote(wui.at[there], place_u, s_exp.at[2, o], s_exp.at[3, o], holder(o)),
-            remote(wdi.at[there], place_d, s_exp.at[4, o], s_exp.at[5, o], holder(o)),
-        )
-
-    def start_experts(o):
-        for copy in expert_copies(o):
+    here_g, here_u, here_d = (d_rows(d), f_rows(r)), (d_rows(d), f_rows(r)), (f_rows(r), d_rows(d))
+    there_g, there_d = (d_rows(1 - d), f_rows(r)), (f_rows(r), d_rows(1 - d))
+
+    def triple(sources, places, first_sem, k, device):
+        return [
+            remote(src, dst, s_exp.at[first_sem + 2 * i, k], s_exp.at[first_sem + 2 * i + 1, k], device)
+            for i, (src, dst) in enumerate(zip(sources, places))
+        ]
+
+    landing = (wg.at[here_g], wu.at[here_u], wd.at[here_d])
+    passed_on = (wg.at[there_g], wu.at[there_g], wd.at[there_d])
+
+    def own_copies(k):
+        return triple((wgi.at[d], wui.at[d], wdi.at[d]), landing, 0, k, tensor(k))
+
+    def across_copies():
+        return triple((wgi.at[1 - d], wui.at[1 - d], wdi.at[1 - d]), landing, 0, 0, partner_dp)
+
+    def passed_copies(k):
+        return triple(passed_on, passed_on, 6, k, tensor(k))
+
+    def start_all(copies):
+        for copy in copies:
             copy.start()
+
+    def wait_recv_all(copies):
+        for copy in copies:
+            copy.wait_recv()
+
+    def wait_send_all(copies):
+        for copy in copies:
+            copy.wait_send()
+
+    loop(1, n_ten, lambda k: start_all(own_copies(k)))
 
     x = xin[...].astype(F32)
     inv = lax.rsqrt(jnp.mean(x * x, axis=-1, keepdims=True) + EPS)
@@ -298,16 +319,15 @@
     def unrope(z):
         return z * cosine - partner(z) * sine
 
-    wg[d_rows(d), f_rows(r)] = wgi[d]
-    wu[d_rows(d), f_rows(r)] = wui[d]
-    wd[f_rows(r), d_rows(d)] = wdi[d]
+    wg[here_g] = wgi[d]
+    wu[here_u] = wui[d]
+    wd[here_d] = wdi[d]
     g_cot = Gather(nq, q, core, plane, sibling, cotall, s_cot)
     cotall[q, core] = cot[wide]
 
     g_wall.forward()
+    start_all(across_copies())
     g_wall.finish()
-    loop(1, n_dp * n_ten, start_experts)
-    g_cot.start()
 
     tails = wall[:, :, :, 768:896].reshape(width, TAIL)
     gains = tails.astype(F32).T
@@ -336,8 +356,11 @@
     columns = lax.broadcasted_iota(jnp.int32, (rows, seq), 1)
     allowed = (columns >= first) & (columns <= row_index)
 
+    wait_recv_all(across_copies())
+    loop(1, n_ten, lambda k: start_all(passed_copies(k)))
     g_kv.forward()
     g_kv.finish()
+    g_cot.start()
 
     o_ref[...] = jnp.zeros_like(o_ref)
 
@@ -366,7 +389,6 @@
         )
 
     loop(1, n_ten, lambda k: tensor_copy(0, s_y1, k).start())
-    g_cot.forward()
     hidden = xin[wide].astype(F32) + part[0, r].astype(F32)
     for k in range(1, n_ten):
         tensor_copy(0, s_y1, k).wait_recv()
@@ -389,14 +411,11 @@
     ).astype(BF16)
     g_ball = Gather(nq, q, core, plane, sibling, ball, s_ball)
     g_ball.start()
+    g_cot.forward()
     g_ball.forward()
+    loop(1, n_ten, lambda k: wait_recv_all(own_copies(k)))
+    loop(1, n_ten, lambda k: wait_recv_all(passed_copies(k)))
     g_cot.finish()
-
-    def wait_experts(o):
-        for copy in expert_copies(o):
-            copy.wait_recv()
-
-    loop(1, n_dp * n_ten, wait_experts)
     g_ball.finish()
 
     expert = 2 * c + d
@@ -446,32 +465,26 @@
     x_ys = Scatter(nq, q, core, plane, sibling, ys, ys_half, ys_land, s_ys)
     x_ys.start()
 
+    def grad_copy(which, table, land, k):
+        place = f_rows(lax.rem(r + k, n_ten))
+        cut_out = table.at[place] if which == 2 else table.at[:, place]
+        return remote(
+            cut_out, land.at[k], s_grad.at[2 * which, k], s_grad.at[2 * which + 1, k], tensor(k)
+        )
+
+    def grad_copies(k):
+        return [
+            grad_copy(0, gg, gg_land, k),
+            grad_copy(1, gu, gu_land, k),
+            grad_copy(2, gd, gd_land, k),
+        ]
+
     all_cot = cotall[...].reshape(nq * 2 * quarter, width)
     all_b = ball[:, :, :, 0:width].reshape(nq * 2 * quarter, width)
     gd[...] = dot_tn(ug_ref[...], all_cot).astype(BF16)
+    loop(1, n_ten, lambda k: grad_copy(2, gd, gd_land, k).start())
     gg[...] = dot_tn(all_b, dgp_ref[...]).astype(BF16)
     gu[...] = dot_tn(all_b, dup_ref[...]).astype(BF16)
-
-    def grad_copies(o):
-        dp, ten = lax.rem(d + o // n_ten, n_dp), lax.rem(r + lax.rem(o, n_ten), n_ten)
-        return (
-            remote(
-                gg.at[d_rows(dp), f_rows(ten)], gg_land.at[o], s_grad.at[0, o], s_grad.at[1, o],
-                holder(o),
-            ),
-            remote(
-                gu.at[d_rows(dp), f_rows(ten)], gu_land.at[o], s_grad.at[2, o], s_grad.at[3, o],
-                holder(o),
-            ),
-            remote(
-                gd.at[f_rows(ten), d_rows(dp)], gd_land.at[o], s_grad.at[4, o], s_grad.at[5, o],
-                holder(o),
-            ),
-        )
-
-    def start_grads(o):
-        for copy in grad_copies(o):
-            copy.start()
 
     summed = x_dbs.total()
     x_ys.send()
@@ -499,9 +512,9 @@
     tail_grad = dot_tn(b_own, dlogits) + dot_tn(ffn_gain_rows, ones_ffn)
     loop(1, n_ten, lambda k: spread(dall, s_dall, k).wait_recv())
 
+    loop(1, n_ten, lambda k: grad_copy(0, gg, gg_land, k).start())
     d_attn = dall[...].reshape(rows, width)
     do = dot(d_attn, w_out).astype(BF16)
-    loop(1, n_dp * n_ten, start_grads)
     for t in range(2):
         tile = do[:, 128 * t : 128 * t + 128].astype(F32)
         for g in range(2):
@@ -575,32 +588,44 @@
         return remote(mine, mine, s_fin.at[2, k], s_fin.at[3, k], tensor(k))
 
     loop(1, n_ten, lambda k: spread_ig(k).start())
+    loop(1, n_ten, lambda k: grad_copy(1, gu, gu_land, k).start())
     x_wgs.send()
 
-    def wait_grads(o):
-        for copy in grad_copies(o):
-            copy.wait_recv()
-
-    loop(1, n_dp * n_ten, wait_grads)
-
-    def reduce_grads(out, land, own):
-        same = own
+    def reduce_grads(table, land, place, land_place):
+        same = table[place].astype(F32)
         for k in range(1, n_ten):
-            same = same + land[k].astype(F32)
-        out[d] = same
-        other = land[n_ten].astype(F32)
-        for k in range(1, n_ten):
-            other = other + land[n_ten + k].astype(F32)
-        out[1 - d] = other
-
-    reduce_grads(o_wg, gg_land, gg[d_rows(d), f_rows(r)].astype(F32))
-    reduce_grads(o_wu, gu_land, gu[d_rows(d), f_rows(r)].astype(F32))
-    reduce_grads(o_wd, gd_land, gd[f_rows(r), d_rows(d)].astype(F32))
+            same = same + land[(k, *land_place)].astype(F32)
+        return same
+
+    sides = ((gg, gg_land, gg_out), (gu, gu_land, gu_out), (gd, gd_land, gd_out))
+    whole = slice(None)
+
+    def half_sum(i, dp):
+        table, land, _ = sides[i]
+        if i == 2:
+            return reduce_grads(table, land, (f_rows(r), d_rows(dp)), (whole, d_rows(dp)))
+        return reduce_grads(table, land, (d_rows(dp), f_rows(r)), (d_rows(dp), whole))
+
+    def half_copy(i):
+        out = sides[i][2]
+        return remote(
+            out.at[0], out.at[1], s_grad.at[2 * i, 0], s_grad.at[2 * i + 1, 0], partner_dp
+        )
+
+    for i, out in ((2, o_wd), (0, o_wg), (1, o_wu)):
+        loop(1, n_ten, lambda k: grad_copy(i, *sides[i][:2], k).wait_recv())
+        sides[i][2][0] = half_sum(i, 1 - d).astype(BF16)
+        half_copy(i).start()
+        out[d] = half_sum(i, d)
 
     loop(1, n_ten, lambda k: spread(hall, s_fin, k).wait_recv())
     o_h[...] = hall[...]
     loop(1, n_ten, lambda k: spread_ig(k).wait_recv())
     o_ig[...] = igall[...].astype(F32)
+
+    for i, out in enumerate((o_wg, o_wu, o_wd)):
+        half_copy(i).wait_recv()
+        out[1 - d] = sides[i][2][1].astype(F32)
 
     grads = x_wgs.total()
     o_w[...] = grads[:, 0:768]
@@ -631,11 +656,16 @@
 
     loop(1, n_ten, drain_tensor)
 
-    def drain_experts(o):
-        for copy in expert_copies(o) + grad_copies(o):
-            copy.wait_send()
-
-    loop(1, n_dp * n_ten, drain_experts)
+    wait_send_all(across_copies())
+
+    def drain_experts(k):
+        wait_send_all(own_copies(k))
+        wait_send_all(passed_copies(k))
+        wait_send_all(grad_copies(k))
+
+    loop(1, n_ten, drain_experts)
+    for i in range(3):
+        half_copy(i).wait_send()
 
 
 def call_layer(sizes, xin, cot, segc, rts, wpk, wgi, wui, wdi):
@@ -649,7 +679,6 @@
     hidden_units = cut * n_ten
     packed = wpk.shape[1]
     all_rows = nq * 2 * quarter
-    holders = n_dp * n_ten
 
     def shape(*dims, kind=F32):
         return jax.ShapeDtypeStruct(dims, kind)
@@ -693,9 +722,12 @@
         low(width, hidden_units),
         low(width, hidden_units),
         low(hidden_units, width),
-        low(holders, half_d, cut),
-        low(holders, half_d, cut),
-        low(holders, cut, half_d),
+        low(n_ten, width, cut),
+        low(n_ten, width, cut),
+        low(n_ten, cut, width),
+        low(2, half_d, cut),
+        low(2, half_d, cut),
+        low(2, cut, half_d),
         low(4, rows, 128),
         full(2, rows, 128),
         low(nj, 2, rows, 256),
@@ -709,11 +741,11 @@
         sems(4, nq),
         sems(4, nq),
         sems(4, nj),
-        sems(6, holders),
+        sems(12, n_ten),
         sems(2, n_ten),
         sems(2, nq),
         sems(2, nq),
-        sems(6, holders),
+        sems(6, n_ten),
         sems(2, n_ten),
         sems(2, nj),
         sems(2, n_ten),

time: 228 us -> 174 us (0.76)
  Pallas kernels: 210 us -> 156 us
    pallas_call x1, Pallas kernels: 210 us -> 156 us  [call_layer(): pl.pallas_call(functools.partial(layer, sizes), out_shape=(shape(n_ten, q...]
where the time goes in v2:
time: 174 us; the launch traced here: 173 us
  Pallas kernels  156 us (90%)
  local copies, waits for them, and re-layouts  15.1 us (9%)
    pallas_call x1, Pallas kernels, call_layer(): pl.pallas_call(functools.partial(layer, sizes), out_shape=(shape(n_ten, q...  156 us
    unnamed x36, local copies, waits for them, and re-layouts  8.96 us

profile of v2, /device:TPU:0, one launch (start us, length us, event | category | flops | bytes accessed | tf_op | source)
XLA Modules:
  0.0 173.5 jit_solution(17398375624347021638)
XLA Ops:
  0.6 0.0 copy-start.12
  0.7 0.6 copy-done.12
  1.3 0.0 copy-start.13
  1.3 0.1 convert_element_type.7
  1.4 0.5 copy-done.13
  2.0 0.0 copy-start.14
  2.0 0.1 copy.31
  2.1 0.6 copy-done.14
  2.6 0.0 copy-start.11
  2.6 0.1 copy.32
  2.7 0.6 copy-done.11
  3.3 0.7 copy.30
  4.0 0.0 copy-start.6
  4.0 0.0 copy-start.7
  4.1 0.7 copy.33.segc
  4.8 0.0 copy-done.6
  4.8 0.0 copy-done.7
  4.8 0.0 copy-start.10
  4.8 0.1 fusion.1
  4.9 0.0 copy-start.8
  4.9 0.0 copy-start.9
  4.9 0.6 copy-done.10
  5.5 0.1 copy-done.8
  5.6 0.0 copy-done.9
  5.6 0.7 concatenate.9.wpk
  6.3 156.2 %shard_map.229 = (bf16[4,32,1024]{2,1,0:T(8,128)(2,1)}, f32[4,32,1024]{2,1,0:T(8,128)}, f32[32,768]{1,0:T(8,128)}, f32[32,128]{1,0:T(8,128)}, f32[2,512,128]{2,1...) custom-call(bf16[128,1024]{1,0:T(8,128)(2,1)} %xin.1, bf16[128,1024]{1,0:T(8,128)(2,1)} %cot.1, ...), custom_call_target="tpu_custom_call" | custom-call | flops 10468982784 | bytes 8388608 | tf_op jit(solution)/shard_map/pallas_call | solution.py:756
  162.5 0.0 copy-start.4
  162.5 1.5 slice_reduce_fusion
  164.0 1.3 slice_bitcast_fusion
  165.4 0.0 copy-start.5
  165.4 0.0 copy-start.3
  165.4 1.4 slice_bitcast_fusion.1
  166.8 0.0 copy-done.4
  166.8 0.1 fusion
  166.9 0.7 maximum_bitcast_fusion.1
  167.6 0.7 maximum_bitcast_fusion
  168.3 0.0 copy-done.5
  168.3 0.7 copy.39
  169.0 0.0 copy-done.3
  169.0 0.0 copy-start.2
  169.0 0.8 copy.40
  169.8 0.4 copy-done.2
  170.2 0.0 copy-start.1
  170.2 0.8 copy.41
  171.0 0.4 copy-done.1
  171.5 0.8 copy.42
  172.2 0.4 copy-done
  172.7 0.8 copy.43
  (3 shorter events, 0.0 us)
Async XLA Ops:
  0.6 0.7 copy-start.12
  1.3 0.7 copy-start.13
  2.0 0.7 copy-start.14
  2.6 0.7 copy-start.11
  4.0 0.7 copy-start.6
  4.0 0.7 copy-start.7
  4.8 0.7 copy-start.10
  4.9 0.7 copy-start.8
  4.9 0.7 copy-start.9
  162.5 4.3 %copy-start.4 = (f32[32,768]{1,0:T(8,128)S(1)}, f32[32,768]{1,0:T(8,128)}, u32[]{:S(2)}) copy-start(f32[32,768]{1,0:T(8,128)} %get-tuple-element.22) | copy-start | bytes 294916
  165.4 2.9 %copy-start.5 = (bf16[4,32,1024]{2,1,0:T(8,128)(2,1)S(1)}, bf16[4,32,1024]{2,1,0:T(8,128)(2,1)}, u32[]{:S(2)}) copy-start(bf16[4,32,1024]{2,1,0:T(8,128)(2,1)} %get-tuple-element.19) | copy-start | bytes 786436
  165.4 3.6 %copy-start.3 = (f32[4,32,1024]{2,1,0:T(8,128)S(1)}, f32[4,32,1024]{2,1,0:T(8,128)}, u32[]{:S(2)}) copy-start(f32[4,32,1024]{2,1,0:T(8,128)} %get-tuple-element.20) | copy-start | bytes 1572868
  169.0 1.2 copy-start.2
  170.2 1.2 copy-start.1
  171.5 1.2 copy-start

commit v3 on v2

--- a/solution.py
+++ b/solution.py
@@ -49,17 +49,18 @@
 
 
 class Gather:
-    def __init__(self, count, me, core, peer, sibling, table, sems):
+    def __init__(self, count, me, core, peer, sibling, table, landed, sems):
         self.count, self.me, self.core = count, me, core
-        self.peer, self.sibling, self.table, self.sems = peer, sibling, table, sems
+        self.peer, self.sibling, self.table = peer, sibling, table
+        self.landed, self.sems = landed, sems
 
     def far(self, k):
         mine = self.table.at[self.me, self.core]
-        return remote(mine, mine, self.sems.at[0, k], self.sems.at[1, k], self.peer(k))
+        return remote(mine, mine, self.sems.at[0], self.landed.at[k], self.peer(k))
 
     def near(self, k):
         chunk = self.table.at[lax.rem(self.me + self.count - k, self.count), self.core]
-        return remote(chunk, chunk, self.sems.at[2, k], self.sems.at[3, k], self.sibling)
+        return remote(chunk, chunk, self.sems.at[1], self.sems.at[2], self.sibling)
 
     def start(self):
         loop(1, self.count, lambda k: self.far(k).start())
@@ -72,12 +73,17 @@
 
         loop(1, self.count, step)
 
+    def near_all(self, side):
+        whole = self.table.at[:, side]
+        return remote(whole, whole, self.sems.at[1], self.sems.at[2], self.sibling)
+
     def finish(self):
-        loop(0, self.count, lambda k: self.near(k).wait_recv())
+        self.near_all(1 - self.core).wait_recv()
 
     def drain(self):
-        loop(1, self.count, lambda k: self.far(k).wait_send())
-        loop(0, self.count, lambda k: self.near(k).wait_send())
+        others = self.table.at[pl.ds(0, self.count - 1), self.core]
+        remote(others, others, self.sems.at[0], self.landed.at[0], self.sibling).wait_send()
+        self.near_all(self.core).wait_send()
 
 
 class Scatter:
@@ -90,8 +96,8 @@
         return remote(
             self.parts.at[:, 1 - self.core],
             self.half,
-            self.sems.at[0, 0],
-            self.sems.at[1, 0],
+            self.sems.at[0],
+            self.sems.at[1],
             self.sibling,
         )
 
@@ -100,9 +106,18 @@
         return remote(
             self.half.at[there],
             self.landed.at[k],
-            self.sems.at[0, k],
-            self.sems.at[1, k],
+            self.sems.at[2],
+            self.sems.at[3],
             self.peer(k),
+        )
+
+    def far_all(self):
+        return remote(
+            self.half.at[pl.ds(1, self.count - 1)],
+            self.landed.at[pl.ds(1, self.count - 1)],
+            self.sems.at[2],
+            self.sems.at[3],
+            self.sibling,
         )
 
     def start(self):
@@ -123,41 +138,60 @@
         add(self.me)
 
     def total(self):
+        self.far_all().wait_recv()
+
         def step(k, acc):
-            self.far(k).wait_recv()
             return acc + self.landed[k].astype(F32)
 
         return lax.fori_loop(1, self.count, step, self.half[self.me].astype(F32))
 
     def drain(self):
         self.near().wait_send()
-        loop(1, self.count, lambda k: self.far(k).wait_send())
+        self.far_all().wait_send()
 
 
 def layer(
     sizes,
     xin,
     cot,
-    segc,
+    seg,
     rts,
-    wpk,
+    gain_a,
+    gain_f,
+    wq,
+    wk,
+    wv,
+    wo,
+    wr,
     wgi,
     wui,
     wdi,
     o_h,
     o_ig,
-    o_w,
+    o_q,
+    o_k,
+    o_v,
+    o_o,
     o_t,
     o_wg,
     o_wu,
     o_wd,
     wall,
+    wall_out,
     cotall,
     ball,
     kv,
     wg,
     wu,
     wd,
+    x_ref,
+    rt_ref,
+    ig_ref,
+    w_ref,
+    t_ref,
+    og_ref,
+    ou_ref,
+    od_ref,
     a_ref,
     qs,
     p_ref,
@@ -191,13 +225,25 @@
     dkv,
     dkv_half,
     dkv_land,
-    wgs,
-    wgs_half,
-    wgs_land,
+    wgo,
+    wgo_half,
+    wgo_land,
+    wgq,
+    wgq_half,
+    wgq_land,
+    wgk,
+    wgk_half,
+    wgk_land,
     tail_y,
+    l_wall,
     s_wall,
+    l_wout,
+    s_wout,
+    l_cot,
     s_cot,
+    l_ball,
     s_ball,
+    l_kv,
     s_kv,
     s_exp,
     s_y1,
@@ -207,8 +253,12 @@
     s_dall,
     s_dkv,
     s_y2,
-    s_wgs,
+    s_wgo,
+    s_wgq,
+    s_wgk,
     s_fin,
+    s_in,
+    s_out,
 ):
     n_dp, n_ctx, n_ten = sizes
     nj = n_ctx // 2
@@ -236,6 +286,18 @@
     partner_dp = at(1 - d, c, r)
     sibling = at(d, c + 1 - 2 * core, r)
 
+    wide = pl.ds(pl.multiple_of(r * quarter, quarter), quarter)
+    half_d, cut = wgi.shape[1], wgi.shape[2]
+
+    def d_rows(dp):
+        return pl.ds(pl.multiple_of(dp * half_d, half_d), half_d)
+
+    def f_rows(ten):
+        return pl.ds(pl.multiple_of(ten * cut, cut), cut)
+
+    here_g, here_u, here_d = (d_rows(d), f_rows(r)), (d_rows(d), f_rows(r)), (f_rows(r), d_rows(d))
+    there_g, there_d = (d_rows(1 - d), f_rows(r)), (f_rows(r), d_rows(1 - d))
+
     barrier = pltpu.get_barrier_semaphore()
 
     def greet(device):
@@ -244,24 +306,59 @@
     loop(1, nq, lambda k: greet(plane(k)))
     greet(sibling)
     loop(1, n_ten, lambda k: greet(tensor(k)))
+
+    loads = [
+        pltpu.make_async_copy(src, dst, s_in.at[i])
+        for i, (src, dst) in enumerate(
+            (
+                (xin, x_ref),
+                (cot.at[wide], cotall.at[q, core]),
+                (wgi.at[d], wg.at[here_g]),
+                (wui.at[d], wu.at[here_u]),
+                (wdi.at[d], wd.at[here_d]),
+            )
+        )
+    ]
+    for load in loads:
+        load.start()
+
+    lane = lax.broadcasted_iota(jnp.int32, (1, 128), 1)
+    group_of = lane // HEAD
+
+    def swap_heads(table):
+        one, two = table[:, 0:128], table[:, 128:256]
+        return (
+            jnp.where(group_of == 0, one, pltpu.roll(two, HEAD, 1)),
+            jnp.where(group_of == 0, pltpu.roll(one, HEAD, 1), two),
+        )
+
+    def diagonal(count, extent, first):
+        up = lax.broadcasted_iota(jnp.int32, (count, extent), 0)
+        return up + first == lax.broadcasted_iota(jnp.int32, (count, extent), 1)
+
+    def as_column(row, count, first):
+        picked = jnp.where(diagonal(count, row.shape[1], first), row, 0.0)
+        return jnp.sum(picked, axis=1, keepdims=True)
+
+    for i, tile in enumerate(swap_heads(wq[...].astype(F32))):
+        wall[q, core, :, 128 * i : 128 * i + 128] = tile.astype(BF16)
+    for i, tile in enumerate(swap_heads(wo[...].astype(F32))):
+        wall_out[q, core, :, 128 * i : 128 * i + 128] = tile.astype(BF16)
+    wall[q, core, :, 256:384] = wk[...]
+    wall[q, core, :, 384:512] = wv[...]
+    numbers_here = seg[...].astype(F32)
+    tail = jnp.where(lane == 32, as_column(gain_a[...].astype(F32), 32, 0), 0.0)
+    tail = jnp.where(lane == 33, as_column(gain_f[...].astype(F32), 32, 0), tail)
+    for i in range(rows // 32):
+        tail = jnp.where(lane == 34 + i, as_column(numbers_here, 32, 32 * i), tail)
+    wall[q, core, :, 512:640] = tail.astype(BF16)
+    wall[q, core, :, 512:544] = wr[...]
+
     pl.semaphore_wait(barrier, nq + n_ten - 1)
 
-    wide = pl.ds(pl.multiple_of(r * quarter, quarter), quarter)
-
-    g_wall = Gather(nq, q, core, plane, sibling, wall, s_wall)
-    wall[q, core] = wpk[...]
+    g_wall = Gather(nq, q, core, plane, sibling, wall, l_wall, s_wall)
     g_wall.start()
-
-    half_d, cut = wgi.shape[1], wgi.shape[2]
-
-    def d_rows(dp):
-        return pl.ds(pl.multiple_of(dp * half_d, half_d), half_d)
-
-    def f_rows(ten):
-        return pl.ds(pl.multiple_of(ten * cut, cut), cut)
-
-    here_g, here_u, here_d = (d_rows(d), f_rows(r)), (d_rows(d), f_rows(r)), (f_rows(r), d_rows(d))
-    there_g, there_d = (d_rows(1 - d), f_rows(r)), (f_rows(r), d_rows(1 - d))
+    g_wout = Gather(nq, q, core, plane, sibling, wall_out, l_wout, s_wout)
 
     def triple(sources, places, first_sem, k, device):
         return [
@@ -278,8 +375,12 @@
     def across_copies():
         return triple((wgi.at[1 - d], wui.at[1 - d], wdi.at[1 - d]), landing, 0, 0, partner_dp)
 
+    def passed_copy(i, k):
+        place = passed_on[i]
+        return remote(place, place, s_exp.at[6 + 2 * i, k], s_exp.at[7 + 2 * i, k], tensor(k))
+
     def passed_copies(k):
-        return triple(passed_on, passed_on, 6, k, tensor(k))
+        return [passed_copy(i, k) for i in range(3)]
 
     def start_all(copies):
         for copy in copies:
@@ -295,11 +396,10 @@
 
     loop(1, n_ten, lambda k: start_all(own_copies(k)))
 
-    x = xin[...].astype(F32)
+    loads[0].wait()
+    x = x_ref[...].astype(F32)
     inv = lax.rsqrt(jnp.mean(x * x, axis=-1, keepdims=True) + EPS)
-    lane = lax.broadcasted_iota(jnp.int32, (1, 128), 1)
     low_half = lax.rem(lane, HEAD) < HEAD // 2
-    group_of = lane // HEAD
     rate = jnp.exp(
         lax.rem(lane, HEAD // 2).astype(F32) * (-2.0 * math.log(10000.0) / HEAD)
     )
@@ -319,17 +419,20 @@
     def unrope(z):
         return z * cosine - partner(z) * sine
 
-    wg[here_g] = wgi[d]
-    wu[here_u] = wui[d]
-    wd[here_d] = wdi[d]
-    g_cot = Gather(nq, q, core, plane, sibling, cotall, s_cot)
-    cotall[q, core] = cot[wide]
+    named = jnp.zeros((128, rows), F32)
+    of_expert = lax.broadcasted_iota(jnp.int32, (128, rows), 0)
+    for k in range(rts.shape[0]):
+        named = named + jnp.where(rts[k : k + 1, :] == of_expert, 1.0, 0.0)
+    rt_ref[...] = named.T
+    for load in loads[1:]:
+        load.wait()
+    g_cot = Gather(nq, q, core, plane, sibling, cotall, l_cot, s_cot)
 
     g_wall.forward()
     start_all(across_copies())
     g_wall.finish()
 
-    tails = wall[:, :, :, 768:896].reshape(width, TAIL)
+    tails = wall[:, :, :, 512:640].reshape(width, TAIL)
     gains = tails.astype(F32).T
     attn_gain, ffn_gain = gains[32:33], gains[33:34]
     a_ref[...] = (x * inv * attn_gain).astype(BF16)
@@ -341,12 +444,13 @@
             qs[2 * t + g] = jnp.where(group_of == g, turned, 0.0).astype(BF16)
     kv[j, core, :, 0:128] = rope(qkv[:, 256:384]).astype(BF16)
     kv[j, core, :, 128:256] = qkv[:, 384:512].astype(BF16)
-    g_kv = Gather(nj, j, core, along, sibling, kv, s_kv)
+    g_kv = Gather(nj, j, core, along, sibling, kv, l_kv, s_kv)
     g_kv.start()
-
-    numbers = wall[pl.ds(d * nj, nj), :, :, 768:896].reshape(nj * 64, TAIL).astype(F32)
+    g_wout.start()
+
+    numbers = wall[pl.ds(d * nj, nj), :, :, 512:640].reshape(nj * 64, TAIL).astype(F32)
     held = jnp.where((lane >= 34) & (lane < 38), numbers, 1e9)
-    mine = segc[...]
+    mine = as_column(numbers_here, rows, 0)
     first = jnp.zeros((rows, 1), F32)
     for s in range(1, 4):
         below = jnp.sum(jnp.where(held < s - 0.5, 1.0, 0.0), axis=0, keepdims=True)
@@ -357,9 +461,10 @@
     allowed = (columns >= first) & (columns <= row_index)
 
     wait_recv_all(across_copies())
-    loop(1, n_ten, lambda k: start_all(passed_copies(k)))
+    loop(1, n_ten, lambda k: passed_copy(0, k).start())
     g_kv.forward()
     g_kv.finish()
+    g_wout.forward()
     g_cot.start()
 
     o_ref[...] = jnp.zeros_like(o_ref)
@@ -375,8 +480,9 @@
         o_ref[i // 2] += jnp.where(group_of == lax.rem(i, 2), out, 0.0)
 
     loop(0, 4, head_forward)
+    g_wout.finish()
     o_low = jnp.concatenate([o_ref[0], o_ref[1]], axis=1).astype(BF16)
-    w_out = wall[:, :, :, 512:768].reshape(width, 256)
+    w_out = wall_out[...].reshape(width, 256)
     part[0] = dot_nt(o_low, w_out).astype(BF16).reshape(n_ten, quarter, width)
 
     def tensor_copy(which, sems, k):
@@ -389,7 +495,7 @@
         )
 
     loop(1, n_ten, lambda k: tensor_copy(0, s_y1, k).start())
-    hidden = xin[wide].astype(F32) + part[0, r].astype(F32)
+    hidden = x_ref[wide].astype(F32) + part[0, r].astype(F32)
     for k in range(1, n_ten):
         tensor_copy(0, s_y1, k).wait_recv()
         hidden = hidden + ybuf[0, k].astype(F32)
@@ -399,18 +505,16 @@
     logits = jnp.where(lane < 32, dot(b_own, tails), NEG)
     expo = jnp.exp(logits - jnp.max(logits, axis=-1, keepdims=True))
     probs = expo / jnp.sum(expo, axis=-1, keepdims=True)
-    routed = jnp.zeros((quarter, 128), F32)
-    routes = rts[wide]
-    for k in range(routes.shape[1]):
-        routed = routed + jnp.where(routes[:, k : k + 1] == lane, 1.0, 0.0)
+    routed = rt_ref[wide]
     gates = probs * routed
     gates_high = gates.astype(BF16).astype(F32)
     ball[q, core, :, 0:width] = b_own
     ball[q, core, :, width : width + TAIL] = (
         gates_high + pltpu.roll(gates - gates_high, 32, 1)
     ).astype(BF16)
-    g_ball = Gather(nq, q, core, plane, sibling, ball, s_ball)
+    g_ball = Gather(nq, q, core, plane, sibling, ball, l_ball, s_ball)
     g_ball.start()
+    loop(1, n_ten, lambda k: start_all([passed_copy(1, k), passed_copy(2, k)]))
     g_cot.forward()
     g_ball.forward()
     loop(1, n_ten, lambda k: wait_recv_all(own_copies(k)))
@@ -487,14 +591,13 @@
     gu[...] = dot_tn(all_b, dup_ref[...]).astype(BF16)
 
     summed = x_dbs.total()
-    x_ys.send()
     dprobs = routed * summed[:, width : width + TAIL]
     dlogits = probs * (dprobs - jnp.sum(probs * dprobs, axis=-1, keepdims=True))
     dlogits = jnp.where(lane < 32, dlogits, 0.0).astype(BF16)
     db = summed[:, 0:width] + dot_nt(dlogits, tails)
     w_db = db * ffn_gain
     grad_hidden = (
-        cot[wide].astype(F32)
+        cotall[q, core].astype(F32)
         + inv_two * w_db
         - hidden * inv_two**3 * (jnp.sum(w_db * hidden, axis=-1, keepdims=True) / width)
     )
@@ -506,6 +609,7 @@
         return remote(mine, mine, sems.at[0, k], sems.at[1, k], tensor(k))
 
     loop(1, n_ten, lambda k: spread(dall, s_dall, k).start())
+    x_ys.send()
     one_hot = lax.broadcasted_iota(jnp.int32, (rows, TAIL), 1)
     ones_ffn = jnp.where(one_hot[0:quarter] == 32, 1.0, 0.0).astype(BF16)
     ones_attn = jnp.where(one_hot == 33, 1.0, 0.0).astype(BF16)
@@ -514,6 +618,13 @@
 
     loop(1, n_ten, lambda k: grad_copy(0, gg, gg_land, k).start())
     d_attn = dall[...].reshape(rows, width)
+
+    def to_rows(grad):
+        return grad.astype(BF16).reshape(nq, 2, 32, grad.shape[1])
+
+    wgo[...] = to_rows(dot_tn(d_attn, o_low))
+    x_wgo = Scatter(nq, q, core, plane, sibling, wgo, wgo_half, wgo_land, s_wgo)
+    x_wgo.start()
     do = dot(d_attn, w_out).astype(BF16)
     for t in range(2):
         tile = do[:, 128 * t : 128 * t + 128].astype(F32)
@@ -521,6 +632,7 @@
             dos[2 * t + g] = jnp.where(group_of == g, tile, 0.0).astype(BF16)
 
     dq_ref[...] = jnp.zeros_like(dq_ref)
+    x_wgo.send()
 
     def head_backward(i):
         go = dos[i]
@@ -544,36 +656,37 @@
     x_dkv = Scatter(nj, j, core, along, sibling, dkv, dkv_half, dkv_land, s_dkv)
     x_dkv.start()
 
-    def to_rows(grad):
-        return grad.astype(BF16).reshape(nq, 2, 32, grad.shape[1])
-
     a_low = a_ref[...]
-    wgs[:, :, :, 512:768] = to_rows(dot_tn(d_attn, o_low))
-    x_dkv.send()
     dq_lin = jnp.concatenate([unrope(dq_ref[0]), unrope(dq_ref[1])], axis=1) * 0.125
     dq_lin = dq_lin.astype(BF16)
-    wgs[:, :, :, 0:256] = to_rows(dot_tn(a_low, dq_lin))
+    x_dkv.send()
+    start_all([grad_copy(1, gu, gu_land, 1), grad_copy(1, gu, gu_land, n_ten - 1)])
+    wgq[...] = to_rows(dot_tn(a_low, dq_lin))
+    x_wgq = Scatter(nq, q, core, plane, sibling, wgq, wgq_half, wgq_land, s_wgq)
+    x_wgq.start()
     da = dot_nt(dq_lin, wall[:, :, :, 0:256].reshape(width, 256))
+    x_wgq.send()
     grad_kv = x_dkv.total()
     dkv_lin = jnp.concatenate([unrope(grad_kv[:, 0:128]), grad_kv[:, 128:256]], axis=1)
     dkv_lin = dkv_lin.astype(BF16)
     da = da + dot_nt(dkv_lin, wall[:, :, :, 256:512].reshape(width, 256))
     part[1] = da.astype(BF16).reshape(n_ten, quarter, width)
     loop(1, n_ten, lambda k: tensor_copy(1, s_y2, k).start())
-    wgs[:, :, :, 256:512] = to_rows(dot_tn(a_low, dkv_lin))
-    attn_gain_rows = (da * xin[...].astype(F32) * inv).astype(BF16)
-    wgs[:, :, :, 768:896] = to_rows(tail_grad + dot_tn(attn_gain_rows, ones_attn))
-    x_wgs = Scatter(nq, q, core, plane, sibling, wgs, wgs_half, wgs_land, s_wgs)
-    x_wgs.start()
+    wgk[:, :, :, 0:256] = to_rows(dot_tn(a_low, dkv_lin))
+    attn_gain_rows = (da * x_ref[...].astype(F32) * inv).astype(BF16)
+    wgk[:, :, :, 256:384] = to_rows(tail_grad + dot_tn(attn_gain_rows, ones_attn))
+    x_wgk = Scatter(nq, q, core, plane, sibling, wgk, wgk_half, wgk_land, s_wgk)
+    x_wgk.start()
 
     hall[r] = (hidden + x_ys.total()).astype(BF16)
+    x_wgk.send()
     loop(1, n_ten, lambda k: spread(hall, s_fin, k).start())
 
     grad_a = part[1, r].astype(F32)
     for k in range(1, n_ten):
         tensor_copy(1, s_y2, k).wait_recv()
         grad_a = grad_a + ybuf[1, k].astype(F32)
-    x_own = xin[wide].astype(F32)
+    x_own = x_ref[wide].astype(F32)
     inv_own = lax.rsqrt(jnp.mean(x_own * x_own, axis=-1, keepdims=True) + EPS)
     w_da = grad_a * attn_gain
     grad_x = (
@@ -588,8 +701,7 @@
         return remote(mine, mine, s_fin.at[2, k], s_fin.at[3, k], tensor(k))
 
     loop(1, n_ten, lambda k: spread_ig(k).start())
-    loop(1, n_ten, lambda k: grad_copy(1, gu, gu_land, k).start())
-    x_wgs.send()
+    loop(2, n_ten - 1, lambda k: grad_copy(1, gu, gu_land, k).start())
 
     def reduce_grads(table, land, place, land_place):
         same = table[place].astype(F32)
@@ -612,38 +724,58 @@
             out.at[0], out.at[1], s_grad.at[2 * i, 0], s_grad.at[2 * i + 1, 0], partner_dp
         )
 
-    for i, out in ((2, o_wd), (0, o_wg), (1, o_wu)):
+    for i, out in ((2, od_ref), (0, og_ref), (1, ou_ref)):
         loop(1, n_ten, lambda k: grad_copy(i, *sides[i][:2], k).wait_recv())
         sides[i][2][0] = half_sum(i, 1 - d).astype(BF16)
         half_copy(i).start()
         out[d] = half_sum(i, d)
 
-    loop(1, n_ten, lambda k: spread(hall, s_fin, k).wait_recv())
-    o_h[...] = hall[...]
-    loop(1, n_ten, lambda k: spread_ig(k).wait_recv())
-    o_ig[...] = igall[...].astype(F32)
-
-    for i, out in enumerate((o_wg, o_wu, o_wd)):
+    stores = []
+
+    def store(src, dst):
+        stores.append(pltpu.make_async_copy(src, dst, s_out.at[len(stores)]))
+        stores[-1].start()
+
+    for i, out, dst in ((2, od_ref, o_wd), (0, og_ref, o_wg), (1, ou_ref, o_wu)):
         half_copy(i).wait_recv()
         out[1 - d] = sides[i][2][1].astype(F32)
-
-    grads = x_wgs.total()
-    o_w[...] = grads[:, 0:768]
-    tail_y[0] = grads[:, 768:896]
+        store(out, dst)
+
+    loop(1, n_ten, lambda k: spread(hall, s_fin, k).wait_recv())
+    store(hall, o_h)
+    loop(1, n_ten, lambda k: spread_ig(k).wait_recv())
+    ig_ref[...] = igall[...].astype(F32)
+    store(ig_ref, o_ig)
+
+    def store_pair(first, total, dst):
+        for i, tile in enumerate(swap_heads(total)):
+            w_ref[:, first + 128 * i : first + 128 * i + 128] = tile
+        store(w_ref.at[:, first : first + 256], dst)
+
+    store_pair(512, x_wgo.total(), o_o)
+    store_pair(0, x_wgq.total(), o_q)
+    grads = x_wgk.total()
+    w_ref[:, 256:512] = grads[:, 0:256]
+    store(w_ref.at[:, 256:384], o_k)
+    store(w_ref.at[:, 384:512], o_v)
+    tail_y[0] = grads[:, 256:384]
 
     def tail_copy(k):
         return remote(tail_y.at[0], tail_y.at[k], s_fin.at[4, k], s_fin.at[5, k], tensor(k))
 
     loop(1, n_ten, lambda k: tail_copy(k).start())
-    tail_sum = grads[:, 768:896]
+    tail_sum = grads[:, 256:384]
     for k in range(1, n_ten):
         tail_copy(k).wait_recv()
         tail_sum = tail_sum + tail_y[k]
-    o_t[...] = tail_sum
-
-    for gather in (g_wall, g_cot, g_kv, g_ball):
+    t_ref[...] = tail_sum
+    store(t_ref, o_t)
+
+    for copy in stores:
+        copy.wait()
+    for gather in (g_wall, g_wout, g_cot, g_kv, g_ball):
         gather.drain()
-    for scatter in (x_dbs, x_ys, x_dkv, x_wgs):
+    for scatter in (x_dbs, x_ys, x_dkv, x_wgo, x_wgq, x_wgk):
         scatter.drain()
 
     def drain_tensor(k):
@@ -668,7 +800,7 @@
         half_copy(i).wait_send()
 
 
-def call_layer(sizes, xin, cot, segc, rts, wpk, wgi, wui, wdi):
+def call_layer(sizes, xin, cot, seg, rts, gain_a, gain_f, wq, wk, wv, wo, wr, wgi, wui, wdi):
     n_dp, n_ctx, n_ten = sizes
     nj = n_ctx // 2
     nq = n_dp * nj
@@ -677,7 +809,6 @@
     quarter = rows // n_ten
     half_d, cut = wgi.shape[1], wgi.shape[2]
     hidden_units = cut * n_ten
-    packed = wpk.shape[1]
     all_rows = nq * 2 * quarter
 
     def shape(*dims, kind=F32):
@@ -693,13 +824,22 @@
         return pltpu.SemaphoreType.DMA(dims)
 
     scratch = [
-        low(nq, 2, 32, packed),
+        low(nq, 2, 32, 640),
+        low(nq, 2, 32, 256),
         low(nq, 2, quarter, width),
         low(nq, 2, quarter, width + TAIL),
         low(nj, 2, rows, 256),
         low(width, hidden_units),
         low(width, hidden_units),
         low(hidden_units, width),
+        low(rows, width),
+        full(rows, 128),
+        full(n_ten, quarter, width),
+        full(32, 768),
+        full(32, TAIL),
+        full(2, half_d, cut),
+        full(2, half_d, cut),
+        full(2, cut, half_d),
         low(rows, width),
         low(4, rows, 128),
         low(4, rows, seq),
@@ -733,50 +873,97 @@
         low(nj, 2, rows, 256),
         low(nj, rows, 256),
         low(nj, rows, 256),
-        low(nq, 2, 32, packed),
-        low(nq, 32, packed),
-        low(nq, 32, packed),
+        low(nq, 2, 32, 256),
+        low(nq, 32, 256),
+        low(nq, 32, 256),
+        low(nq, 2, 32, 256),
+        low(nq, 32, 256),
+        low(nq, 32, 256),
+        low(nq, 2, 32, 384),
+        low(nq, 32, 384),
+        low(nq, 32, 384),
         full(n_ten, 32, TAIL),
-        sems(4, nq),
-        sems(4, nq),
-        sems(4, nq),
-        sems(4, nj),
+        sems(nq),
+        sems(3),
+        sems(nq),
+        sems(3),
+        sems(nq),
+        sems(3),
+        sems(nq),
+        sems(3),
+        sems(nj),
+        sems(3),
         sems(12, n_ten),
         sems(2, n_ten),
-        sems(2, nq),
-        sems(2, nq),
+        sems(4),
+        sems(4),
         sems(6, n_ten),
         sems(2, n_ten),
-        sems(2, nj),
+        sems(4),
         sems(2, n_ten),
-        sems(2, nq),
+        sems(4),
+        sems(4),
+        sems(4),
         sems(6, n_ten),
+        sems(5),
+        sems(10),
     ]
+    far, near = pl.BlockSpec(memory_space=pltpu.HBM), pl.BlockSpec(memory_space=pltpu.VMEM)
     flops = 2 * (9 * all_rows * width * hidden_units + 4 * rows * width * 768)
     return pl.pallas_call(
         functools.partial(layer, sizes),
         out_shape=(
             shape(n_ten, quarter, width, kind=BF16),
             shape(n_ten, quarter, width),
-            shape(32, 768),
+            shape(32, 256),
+            shape(32, 128),
+            shape(32, 128),
+            shape(32, 256),
             shape(32, TAIL),
             shape(2, half_d, cut),
             shape(2, half_d, cut),
             shape(2, cut, half_d),
         ),
-        in_specs=[pl.BlockSpec(memory_space=pltpu.VMEM)] * 8,
-        out_specs=[pl.BlockSpec(memory_space=pltpu.VMEM)] * 7,
+        in_specs=[far, far] + [near] * 9 + [far] * 3,
+        out_specs=[far] * 10,
         scratch_shapes=scratch,
         compiler_params=pltpu.CompilerParams(
             collective_id=0, has_side_effects=True, vmem_limit_bytes=VMEM_BYTES
         ),
         cost_estimate=pl.CostEstimate(flops=flops, bytes_accessed=8 << 20, transcendentals=0),
-    )(xin, cot, segc, rts, wpk, wgi, wui, wdi)
-
-
-def swap_heads(table):
-    a, b, c, d = [table[:, HEAD * i : HEAD * i + HEAD] for i in range(4)]
-    return jnp.concatenate([a, c, b, d], axis=1)
+    )(xin, cot, seg, rts, gain_a, gain_f, wq, wk, wv, wo, wr, wgi, wui, wdi)
+
+
+def hand_over(*refs):
+    sources, tail = refs[:9], refs[9]
+    results, gain_a, gain_f, router, sems = refs[10:19], *refs[19:]
+    copies = [
+        pltpu.make_async_copy(src, dst, sems.at[i])
+        for i, (src, dst) in enumerate(zip(sources, results))
+    ]
+    for copy in copies:
+        copy.start()
+    router[...] = tail[:, 0:32]
+    up = lax.broadcasted_iota(jnp.int32, (32, 32), 0)
+    same = up == lax.broadcasted_iota(jnp.int32, (32, 32), 1)
+    gain_a[...] = jnp.sum(jnp.where(same, tail[:, 33:34], 0.0), axis=0, keepdims=True)
+    gain_f[...] = jnp.sum(jnp.where(same, tail[:, 32:33], 0.0), axis=0, keepdims=True)
+    for copy in copies:
+        copy.wait()
+
+
+def call_hand_over(arrays, tail):
+    far, near = pl.BlockSpec(memory_space=pltpu.HBM), pl.BlockSpec(memory_space=pltpu.VMEM)
+    small = [(1, 32), (1, 32), (32, 32)]
+    return pl.pallas_call(
+        hand_over,
+        out_shape=[jax.ShapeDtypeStruct(a.shape, a.dtype) for a in arrays]
+        + [jax.ShapeDtypeStruct(dims, F32) for dims in small],
+        in_specs=[near] * (len(arrays) + 1),
+        out_specs=[far] * len(arrays) + [near] * 3,
+        scratch_shapes=[pltpu.SemaphoreType.DMA((len(arrays),))],
+        compiler_params=pltpu.CompilerParams(vmem_limit_bytes=VMEM_BYTES),
+    )(*arrays, tail)
 
 
 def per_device(
@@ -796,43 +983,46 @@
     cotangent,
 ):
     sizes = (lax.axis_size("dp"), lax.axis_size("context"), lax.axis_size("tensor"))
-    rows = hidden_in.shape[0]
-    per_row = rows // 32
-    packed = jnp.concatenate(
-        [
-            swap_heads(w_query[0]),
-            w_key[0],
-            w_value[0],
-            swap_heads(w_out[0].T),
-            w_router[0],
-            norm_attn[0][:, None],
-            norm_ffn[0][:, None],
-            segments[0].reshape(32, per_row).astype(BF16),
-            jnp.zeros((32, TAIL - 34 - per_row), BF16),
-        ],
-        axis=1,
-    )
-    out, grad, w_grads, tail, gate_grad, up_grad, down_grad = call_layer(
+    out, grad, wq, wk, wv, wo, tail, gate_grad, up_grad, down_grad = call_layer(
         sizes,
         hidden_in,
         cotangent,
-        segments[0][:, None],
-        routes[0],
-        packed,
+        segments,
+        routes[0].T,
+        norm_attn,
+        norm_ffn,
+        w_query[0],
+        w_key[0],
+        w_value[0],
+        w_out[0].T,
+        w_router[0],
         w_gate[0],
         w_up[0],
         w_down[0],
     )
-    return (
+    arrays = (
         out.reshape(hidden_in.shape),
         grad.reshape(hidden_in.shape),
-        tail[:, 33][None],
-        swap_heads(w_grads[:, 0:256])[None],
-        w_grads[:, 256:384][None],
-        w_grads[:, 384:512][None],
-        swap_heads(w_grads[:, 512:768]).T[None],
-        tail[:, 32][None],
-        tail[:, 0:32][None],
+        wq,
+        wk,
+        wv,
+        wo,
+        gate_grad,
+        up_grad,
+        down_grad,
+    )
+    results = call_hand_over(arrays, tail)
+    out, grad, wq, wk, wv, wo, gate_grad, up_grad, down_grad, gain_a, gain_f, router = results
+    return (
+        out,
+        grad,
+        gain_a,
+        wq[None],
+        wk[None],
+        wv[None],
+        wo.T[None],
+        gain_f,
+        router[None],
         gate_grad[None],
         up_grad[None],
         down_grad[None],

time: 174 us -> 152 us (0.87)
  local copies, waits for them, and re-layouts: 15.1 us -> 0 us
  Pallas kernels: 156 us -> 151 us
    pallas_call x1, Pallas kernels: 156 us -> 147 us  [call_layer(): pl.pallas_call(functools.partial(layer, sizes), out_shape=(shape(n_ten, q...]
    unnamed x36 -> x0, local copies, waits for them, and re-layouts: 8.96 us -> none
    pallas_call x0 -> x1, Pallas kernels: none -> 3.78 us  [call_hand_over(): pl.pallas_call(hand_over, out_shape=[jax.ShapeDtypeStruct(a.shape, a.dtyp...]
    broadcast_in_dim x3 -> x0, local copies, waits for them, and re-layouts: 2.75 us -> none  [the longest x1 1.42 us: per_device(): w_grads[:, 384:512][None]]
where the time goes in v3:
time: 152 us; the launch traced here: 151 us
  Pallas kernels  151 us (99%)
    pallas_call x1, Pallas kernels, call_layer(): pl.pallas_call(functools.partial(layer, sizes), out_shape=(shape(n_ten, q...  147 us
    pallas_call x1, Pallas kernels, call_hand_over(): pl.pallas_call(hand_over, out_shape=[jax.ShapeDtypeStruct(a.shape, a.dtyp...  3.78 us

profile of v3, /device:TPU:0, one launch (start us, length us, event | category | flops | bytes accessed | tf_op | source)
XLA Modules:
  0.0 151.3 jit_solution(14232786628259596282)
XLA Ops:
  0.6 146.8 %shard_map.229 = (bf16[4,32,1024]{2,1,0:T(8,128)(2,1)}, f32[4,32,1024]{2,1,0:T(8,128)}, f32[32,256]{1,0:T(8,128)}, f32[32,128]{1,0:T(8,128)}, f32[32,128]{1,0:T(...) custom-call(bf16[128,1024]{1,0:T(8,128)(2,1)} %xin.1, ...), custom_call_target="tpu_custom_call" | custom-call | flops 10468982784 | bytes 8388608 | tf_op jit(solution)/shard_map/pallas_call | solution.py:913
  147.5 3.8 %shard_map.230 = (bf16[128,1024]{1,0:T(8,128)(2,1)}, f32[128,1024]{1,0:T(8,128)}, f32[32,256]{1,0:T(8,128)}, f32[32,128]{1,0:T(8,128)}, f32[32,128]{1,0:T(8,128)...) custom-call(bf16[128,1024]{1,0:T(8,128)(2,1)} %bitcast.26, ...), custom_call_target="tpu_custom_call" | custom-call | tf_op jit(solution)/shard_map/pallas_call | solution.py:958

commit v4 on v3

--- a/solution.py
+++ b/solution.py
@@ -148,6 +148,190 @@
     def drain(self):
         self.near().wait_send()
         self.far_all().wait_send()
+
+
+class Plane:
+    def __init__(self, d, x, zh, nx, core, sibling, x_peer, z_peer):
+        self.d, self.x, self.zh, self.nx = d, x, zh, nx
+        self.core, self.sibling = core, sibling
+        self.x_peer, self.z_peer = x_peer, z_peer
+
+    def x_at(self, k):
+        return lax.rem(self.x + k + self.nx, self.nx)
+
+    def z_at(self, k):
+        z = lax.rem(2 * self.d + self.zh + k + 4, 4)
+        return z // 2, lax.rem(z, 2)
+
+
+def upper(rows):
+    return pl.ds(0, rows // 2)
+
+
+def lower(rows):
+    return pl.ds(rows // 2, rows // 2)
+
+
+class PlaneGather:
+    def __init__(self, plane, table, landed, sems):
+        self.plane, self.table, self.landed, self.sems = plane, table, landed, sems
+        rows = table.shape[4]
+        self.up, self.down = upper(rows), lower(rows)
+
+    def line(self, k):
+        d, zh = self.plane.z_at(k)
+        return self.table.at[d, :, zh, self.plane.core, self.up]
+
+    def column(self, k):
+        return self.table.at[:, self.plane.x_at(k), :, self.plane.core, self.down]
+
+    def send(self, part, stage, k, device):
+        remote(part, part, self.sems.at[stage], self.landed.at[stage, k], device).start()
+
+    def landing(self, part, stage, k):
+        return remote(
+            part, part, self.sems.at[stage], self.landed.at[stage, k], self.plane.sibling
+        )
+
+    def pass_on(self, k):
+        for part in (self.line(-k), self.column(-k)):
+            remote(part, part, self.sems.at[2], self.sems.at[3], self.plane.sibling).start()
+
+    def start(self):
+        p = self.plane
+        chunk = self.table.at[p.d, p.x, p.zh, p.core]
+
+        def step(k):
+            self.send(chunk.at[self.up], 0, k, p.x_peer(k))
+            self.send(chunk.at[self.down], 0, k, p.z_peer(k))
+
+        loop(1, p.nx, step)
+
+    def forward(self):
+        p = self.plane
+        loop(1, p.nx, lambda k: self.landing(self.table.at[0, 0, 0, p.core], 0, k).wait_recv())
+
+        def step(k):
+            self.send(self.line(0), 1, k, p.z_peer(k))
+            self.send(self.column(0), 1, k, p.x_peer(k))
+
+        loop(1, p.nx, step)
+        self.pass_on(0)
+
+    def forward_rest(self):
+        p = self.plane
+
+        def arrive(k):
+            self.landing(self.table.at[0, :, 0, p.core], 1, k).wait_recv()
+            self.pass_on(k)
+
+        loop(1, p.nx, arrive)
+
+    def near_all(self, side):
+        whole = self.table.at[:, :, :, side]
+        return remote(whole, whole, self.sems.at[2], self.sems.at[3], self.plane.sibling)
+
+    def finish(self):
+        self.near_all(1 - self.plane.core).wait_recv()
+
+    def drain(self):
+        core, others = self.plane.core, pl.ds(0, self.plane.nx - 1)
+        self.landing(self.table.at[0, others, 0, core], 0, 0).wait_send()
+        self.landing(self.table.at[:, others, :, core], 1, 0).wait_send()
+        self.near_all(core).wait_send()
+
+
+class PlaneScatter:
+    def __init__(self, plane, parts, half, line, column, last, landed, sems):
+        self.plane, self.parts, self.half = plane, parts, half
+        self.line, self.column, self.last = line, column, last
+        self.landed, self.sems = landed, sems
+        rows = parts.shape[4]
+        self.up, self.down = upper(rows), lower(rows)
+
+    def copy(self, src, dst, stage, k, device):
+        return remote(src, dst, self.sems.at[stage], self.landed.at[stage, k], device)
+
+    def near(self):
+        p = self.plane
+        away = self.parts.at[:, :, :, 1 - p.core]
+        return remote(away, self.half, self.sems.at[2], self.sems.at[3], p.sibling)
+
+    def start(self):
+        self.near().start()
+
+    def send(self):
+        p = self.plane
+        self.near().wait_recv()
+
+        def add(i):
+            spot = (i // (2 * p.nx), lax.rem(i // 2, p.nx), lax.rem(i, 2))
+            mine = self.parts[(*spot, p.core)].astype(F32)
+            self.half[spot] = (mine + self.half[spot].astype(F32)).astype(BF16)
+
+        loop(0, 4 * p.nx, add)
+
+        def step(k):
+            d, zh = p.z_at(k)
+            there = self.half.at[d, :, zh, self.up]
+            self.copy(there, self.line.at[k], 0, k, p.z_peer(k)).start()
+            there = self.half.at[:, p.x_at(k), :, self.down]
+            self.copy(there, self.column.at[k], 0, k, p.x_peer(k)).start()
+
+        loop(1, p.nx, step)
+
+    def middle(self):
+        p = self.plane
+
+        def arrive(k):
+            two = self.line.at[pl.ds(0, 2)]
+            self.copy(two, two, 0, k, p.sibling).wait_recv()
+
+        loop(1, p.nx, arrive)
+
+        def add_line(k):
+            spot = (p.d, p.x_at(k), p.zh, self.up)
+            total = self.half[spot].astype(F32)
+            for i in range(1, p.nx):
+                total = total + self.line[i, p.x_at(k)].astype(F32)
+            self.half[spot] = total.astype(BF16)
+
+        def add_column(k):
+            d, zh = p.z_at(k)
+            spot = (d, p.x, zh, self.down)
+            total = self.half[spot].astype(F32)
+            for i in range(1, p.nx):
+                total = total + self.column[i, d, zh].astype(F32)
+            self.half[spot] = total.astype(BF16)
+
+        def step(k):
+            add_line(k)
+            spot = self.half.at[p.d, p.x_at(k), p.zh, self.up]
+            self.copy(spot, self.last.at[k, self.up], 1, k, p.x_peer(k)).start()
+            add_column(k)
+            d, zh = p.z_at(k)
+            spot = self.half.at[d, p.x, zh, self.down]
+            self.copy(spot, self.last.at[k, self.down], 1, k, p.z_peer(k)).start()
+
+        loop(1, p.nx, step)
+        add_line(0)
+        add_column(0)
+
+    def total(self):
+        p = self.plane
+        total = self.half[p.d, p.x, p.zh].astype(F32)
+        for k in range(1, p.nx):
+            self.copy(self.last.at[k], self.last.at[k], 1, k, p.sibling).wait_recv()
+            total = total + self.last[k].astype(F32)
+        return total
+
+    def drain(self):
+        p, others = self.plane, pl.ds(0, self.plane.nx - 1)
+        self.near().wait_send()
+        first = self.half.at[:, others]
+        self.copy(first, first, 0, 0, p.sibling).wait_send()
+        second = self.half.at[0, others, 0]
+        self.copy(second, second, 1, 0, p.sibling).wait_send()
 
 
 def layer(
@@ -207,16 +391,23 @@
     ug_ref,
     dbs,
     dbs_half,
-    dbs_land,
+    dbs_line,
+    dbs_column,
+    dbs_last,
     ys,
     ys_half,
-    ys_land,
+    ys_line,
+    ys_column,
+    ys_last,
     gg,
     gu,
     gd,
     gg_land,
     gu_land,
     gd_land,
+    gg_relay,
+    gu_relay,
+    gd_relay,
     gg_out,
     gu_out,
     gd_out,
@@ -227,13 +418,19 @@
     dkv_land,
     wgo,
     wgo_half,
-    wgo_land,
+    wgo_line,
+    wgo_column,
+    wgo_last,
     wgq,
     wgq_half,
-    wgq_land,
+    wgq_line,
+    wgq_column,
+    wgq_last,
     wgk,
     wgk_half,
-    wgk_land,
+    wgk_line,
+    wgk_column,
+    wgk_last,
     tail_y,
     l_wall,
     s_wall,
@@ -247,14 +444,19 @@
     s_kv,
     s_exp,
     s_y1,
+    l_dbs,
     s_dbs,
+    l_ys,
     s_ys,
     s_grad,
     s_dall,
     s_dkv,
     s_y2,
+    l_wgo,
     s_wgo,
+    l_wgq,
     s_wgq,
+    l_wgk,
     s_wgk,
     s_fin,
     s_in,
@@ -268,14 +470,19 @@
     quarter = rows // n_ten
     d, c, r = lax.axis_index("dp"), lax.axis_index("context"), lax.axis_index("tensor")
     core, j = lax.rem(c, 2), c // 2
-    q = d * nj + j
 
     def at(dp, context, tensor):
         return {"dp": dp, "context": context, "tensor": tensor}
 
-    def plane(k):
-        there = lax.rem(q + k, nq)
-        return at(there // nj, lax.rem(there, nj) * 2 + core, r)
+    nx = nj // 2
+    x_here, zh = j // 2, lax.rem(j, 2)
+
+    def x_peer(k):
+        return at(d, (lax.rem(x_here + k, nx) * 2 + zh) * 2 + core, r)
+
+    def z_peer(k):
+        z = lax.rem(2 * d + zh + k, 4)
+        return at(z // 2, (x_here * 2 + lax.rem(z, 2)) * 2 + core, r)
 
     def along(k):
         return at(d, lax.rem(j + k, nj) * 2 + core, r)
@@ -285,6 +492,8 @@
 
     partner_dp = at(1 - d, c, r)
     sibling = at(d, c + 1 - 2 * core, r)
+    plane = Plane(d, x_here, zh, nx, core, sibling, x_peer, z_peer)
+    own = (d, x_here, zh, core)
 
     wide = pl.ds(pl.multiple_of(r * quarter, quarter), quarter)
     half_d, cut = wgi.shape[1], wgi.shape[2]
@@ -303,7 +512,8 @@
     def greet(device):
         pl.semaphore_signal(barrier, inc=1, device_id=device, device_id_type=pl.DeviceIdType.MESH)
 
-    loop(1, nq, lambda k: greet(plane(k)))
+    loop(1, nj, lambda k: greet(along(k)))
+    loop(1, nx, lambda k: greet(z_peer(k)))
     greet(sibling)
     loop(1, n_ten, lambda k: greet(tensor(k)))
 
@@ -312,7 +522,7 @@
         for i, (src, dst) in enumerate(
             (
                 (xin, x_ref),
-                (cot.at[wide], cotall.at[q, core]),
+                (cot.at[wide], cotall.at[own]),
                 (wgi.at[d], wg.at[here_g]),
                 (wui.at[d], wu.at[here_u]),
                 (wdi.at[d], wd.at[here_d]),
@@ -341,24 +551,24 @@
         return jnp.sum(picked, axis=1, keepdims=True)
 
     for i, tile in enumerate(swap_heads(wq[...].astype(F32))):
-        wall[q, core, :, 128 * i : 128 * i + 128] = tile.astype(BF16)
+        wall[(*own, slice(None), slice(128 * i, 128 * i + 128))] = tile.astype(BF16)
     for i, tile in enumerate(swap_heads(wo[...].astype(F32))):
-        wall_out[q, core, :, 128 * i : 128 * i + 128] = tile.astype(BF16)
-    wall[q, core, :, 256:384] = wk[...]
-    wall[q, core, :, 384:512] = wv[...]
+        wall_out[(*own, slice(None), slice(128 * i, 128 * i + 128))] = tile.astype(BF16)
+    wall[(*own, slice(None), slice(256, 384))] = wk[...]
+    wall[(*own, slice(None), slice(384, 512))] = wv[...]
     numbers_here = seg[...].astype(F32)
     tail = jnp.where(lane == 32, as_column(gain_a[...].astype(F32), 32, 0), 0.0)
     tail = jnp.where(lane == 33, as_column(gain_f[...].astype(F32), 32, 0), tail)
     for i in range(rows // 32):
         tail = jnp.where(lane == 34 + i, as_column(numbers_here, 32, 32 * i), tail)
-    wall[q, core, :, 512:640] = tail.astype(BF16)
-    wall[q, core, :, 512:544] = wr[...]
-
-    pl.semaphore_wait(barrier, nq + n_ten - 1)
-
-    g_wall = Gather(nq, q, core, plane, sibling, wall, l_wall, s_wall)
+    wall[(*own, slice(None), slice(512, 640))] = tail.astype(BF16)
+    wall[(*own, slice(None), slice(512, 544))] = wr[...]
+
+    pl.semaphore_wait(barrier, nj + nx + n_ten - 2)
+
+    g_wall = PlaneGather(plane, wall, l_wall, s_wall)
     g_wall.start()
-    g_wout = Gather(nq, q, core, plane, sibling, wall_out, l_wout, s_wout)
+    g_wout = PlaneGather(plane, wall_out, l_wout, s_wout)
 
     def triple(sources, places, first_sem, k, device):
         return [
@@ -368,6 +578,7 @@
 
     landing = (wg.at[here_g], wu.at[here_u], wd.at[here_d])
     passed_on = (wg.at[there_g], wu.at[there_g], wd.at[there_d])
+    sides_y = (1, n_ten - 1)
 
     def own_copies(k):
         return triple((wgi.at[d], wui.at[d], wdi.at[d]), landing, 0, k, tensor(k))
@@ -382,6 +593,18 @@
     def passed_copies(k):
         return [passed_copy(i, k) for i in range(3)]
 
+    def relay_copies(dp, first_sem, side):
+        ten = lax.rem(r + sides_y[1 - side], n_ten)
+        step, narrow = half_d // 2, cut // 2
+        d_half = pl.ds(pl.multiple_of(dp * half_d + side * step, step), step)
+        f_half = pl.ds(pl.multiple_of(ten * cut + side * narrow, narrow), narrow)
+        parts = (
+            wg.at[d_half, f_rows(ten)],
+            wu.at[d_half, f_rows(ten)],
+            wd.at[f_half, d_rows(dp)],
+        )
+        return triple(parts, parts, first_sem, n_ten + side, tensor(sides_y[side]))
+
     def start_all(copies):
         for copy in copies:
             copy.start()
@@ -394,7 +617,8 @@
         for copy in copies:
             copy.wait_send()
 
-    loop(1, n_ten, lambda k: start_all(own_copies(k)))
+    for k in sides_y:
+        start_all(own_copies(k))
 
     loads[0].wait()
     x = x_ref[...].astype(F32)
@@ -426,18 +650,23 @@
     rt_ref[...] = named.T
     for load in loads[1:]:
         load.wait()
-    g_cot = Gather(nq, q, core, plane, sibling, cotall, l_cot, s_cot)
+    g_cot = PlaneGather(plane, cotall, l_cot, s_cot)
 
     g_wall.forward()
+    g_wall.forward_rest()
     start_all(across_copies())
     g_wall.finish()
-
-    tails = wall[:, :, :, 512:640].reshape(width, TAIL)
+    for k in sides_y:
+        wait_recv_all(own_copies(k))
+    for side in range(2):
+        start_all(relay_copies(d, 0, side))
+
+    tails = wall[:, :, :, :, :, 512:640].reshape(width, TAIL)
     gains = tails.astype(F32).T
     attn_gain, ffn_gain = gains[32:33], gains[33:34]
     a_ref[...] = (x * inv * attn_gain).astype(BF16)
 
-    qkv = dot(a_ref[...], wall[:, :, :, 0:512].reshape(width, 512))
+    qkv = dot(a_ref[...], wall[:, :, :, :, :, 0:512].reshape(width, 512))
     for t in range(2):
         turned = rope(qkv[:, 128 * t : 128 * t + 128]) * 0.125
         for g in range(2):
@@ -448,7 +677,7 @@
     g_kv.start()
     g_wout.start()
 
-    numbers = wall[pl.ds(d * nj, nj), :, :, 512:640].reshape(nj * 64, TAIL).astype(F32)
+    numbers = wall[d, :, :, :, :, 512:640].reshape(nj * 64, TAIL).astype(F32)
     held = jnp.where((lane >= 34) & (lane < 38), numbers, 1e9)
     mine = as_column(numbers_here, rows, 0)
     first = jnp.zeros((rows, 1), F32)
@@ -460,11 +689,13 @@
     columns = lax.broadcasted_iota(jnp.int32, (rows, seq), 1)
     allowed = (columns >= first) & (columns <= row_index)
 
+    g_kv.forward()
+    g_wout.forward()
+    g_wout.forward_rest()
+    g_kv.finish()
     wait_recv_all(across_copies())
-    loop(1, n_ten, lambda k: passed_copy(0, k).start())
-    g_kv.forward()
-    g_kv.finish()
-    g_wout.forward()
+    for k in sides_y:
+        passed_copy(0, k).start()
     g_cot.start()
 
     o_ref[...] = jnp.zeros_like(o_ref)
@@ -508,27 +739,39 @@
     routed = rt_ref[wide]
     gates = probs * routed
     gates_high = gates.astype(BF16).astype(F32)
-    ball[q, core, :, 0:width] = b_own
-    ball[q, core, :, width : width + TAIL] = (
+    ball[(*own, slice(None), slice(0, width))] = b_own
+    ball[(*own, slice(None), slice(width, width + TAIL))] = (
         gates_high + pltpu.roll(gates - gates_high, 32, 1)
     ).astype(BF16)
-    g_ball = Gather(nq, q, core, plane, sibling, ball, l_ball, s_ball)
+    g_ball = PlaneGather(plane, ball, l_ball, s_ball)
     g_ball.start()
-    loop(1, n_ten, lambda k: start_all([passed_copy(1, k), passed_copy(2, k)]))
+    for k in sides_y:
+        start_all([passed_copy(1, k), passed_copy(2, k)])
     g_cot.forward()
+    g_cot.forward_rest()
     g_ball.forward()
-    loop(1, n_ten, lambda k: wait_recv_all(own_copies(k)))
-    loop(1, n_ten, lambda k: wait_recv_all(passed_copies(k)))
+    for k in sides_y:
+        wait_recv_all(passed_copies(k))
+    for side in range(2):
+        start_all(relay_copies(1 - d, 6, side))
+    g_ball.forward_rest()
+    for side in range(2):
+        wait_recv_all(relay_copies(d, 0, side))
+        wait_recv_all(relay_copies(1 - d, 6, side))
     g_cot.finish()
     g_ball.finish()
 
     expert = 2 * c + d
     gate_lane = (lane == expert) | (lane == expert + 32)
     block = 8 * quarter
-    steps = nq // 4
+    steps = 4
+
+    def place_of(i):
+        whole = slice(None)
+        return (i // 2, pl.ds(2 * lax.rem(i, 2), 2), whole, whole, whole)
 
     def tokens(ref, i, cut_at, cut_to):
-        return ref[pl.ds(4 * i, 4), :, :, cut_at:cut_to].reshape(block, cut_to - cut_at)
+        return ref[(*place_of(i), slice(cut_at, cut_to))].reshape(block, cut_to - cut_at)
 
     def rows_of(i):
         return pl.ds(pl.multiple_of(i * block, block), block)
@@ -551,44 +794,84 @@
         dup_ref[rows_of(i)] = dup
         ug_ref[rows_of(i)] = (gate * u).astype(BF16)
         db = dot_nt(dgp, wg[...]) + dot_nt(dup, wu[...])
-        dbs[pl.ds(4 * i, 4), :, :, 0:width] = db.astype(BF16).reshape(4, 2, quarter, width)
-        dbs[pl.ds(4 * i, 4), :, :, width : width + TAIL] = (
-            jnp.where(lane == expert, dgate, 0.0).astype(BF16).reshape(4, 2, quarter, TAIL)
+        dbs[(*place_of(i), slice(0, width))] = db.astype(BF16).reshape(2, 2, 2, quarter, width)
+        dbs[(*place_of(i), slice(width, width + TAIL))] = (
+            jnp.where(lane == expert, dgate, 0.0).astype(BF16).reshape(2, 2, 2, quarter, TAIL)
         )
 
     loop(0, steps, expert_block)
-    x_dbs = Scatter(nq, q, core, plane, sibling, dbs, dbs_half, dbs_land, s_dbs)
+    x_dbs = PlaneScatter(plane, dbs, dbs_half, dbs_line, dbs_column, dbs_last, l_dbs, s_dbs)
     x_dbs.start()
 
     def down_block(i):
         y = dot(ug_ref[rows_of(i)], wd[...])
-        ys[pl.ds(4 * i, 4)] = y.astype(BF16).reshape(4, 2, quarter, width)
+        ys[place_of(i)] = y.astype(BF16).reshape(2, 2, 2, quarter, width)
 
     loop(0, steps, down_block)
     x_dbs.send()
-    x_ys = Scatter(nq, q, core, plane, sibling, ys, ys_half, ys_land, s_ys)
+    x_ys = PlaneScatter(plane, ys, ys_half, ys_line, ys_column, ys_last, l_ys, s_ys)
     x_ys.start()
 
-    def grad_copy(which, table, land, k):
-        place = f_rows(lax.rem(r + k, n_ten))
-        cut_out = table.at[place] if which == 2 else table.at[:, place]
-        return remote(
-            cut_out, land.at[k], s_grad.at[2 * which, k], s_grad.at[2 * which + 1, k], tensor(k)
-        )
-
-    def grad_copies(k):
-        return [
-            grad_copy(0, gg, gg_land, k),
-            grad_copy(1, gu, gu_land, k),
-            grad_copy(2, gd, gd_land, k),
-        ]
+    tables = ((gg, gg_land, gg_relay, gg_out), (gu, gu_land, gu_relay, gu_out), (gd, gd_land, gd_relay, gd_out))
+
+    def grad_place(i, dp, ten):
+        return (f_rows(ten), d_rows(dp)) if i == 2 else (d_rows(dp), f_rows(ten))
+
+    def relay_grad(i, side):
+        table, _, relay, _ = tables[i]
+        part = table.at[grad_place(i, side, lax.rem(r + 2, n_ten))]
+        sems = s_grad.at[2 * i, n_ten + side], s_grad.at[2 * i + 1, n_ten + side]
+        return remote(part, relay.at[side], *sems, tensor(sides_y[side]))
+
+    def grad_copy(i, side):
+        table, land = tables[i][:2]
+        k = sides_y[side]
+        ten = lax.rem(r + k, n_ten)
+        part = table.at[f_rows(ten)] if i == 2 else table.at[:, f_rows(ten)]
+        sems = s_grad.at[2 * i, k], s_grad.at[2 * i + 1, k]
+        return remote(part, land.at[side], *sems, tensor(k))
+
+    def start_relays(i):
+        for side in range(2):
+            relay_grad(i, side).start()
+
+    def start_grads(i):
+        table, _, relay, _ = tables[i]
+        for side in range(2):
+            relay_grad(i, side).wait_recv()
+            place = grad_place(i, side, lax.rem(r + sides_y[side], n_ten))
+            table[place] = (table[place].astype(F32) + relay[side].astype(F32)).astype(BF16)
+            grad_copy(i, side).start()
+
+    def half_sum(i, dp):
+        table, land = tables[i][:2]
+        total = table[grad_place(i, dp, r)].astype(F32)
+        for side in range(2):
+            part = land[side, :, d_rows(dp)] if i == 2 else land[side, d_rows(dp)]
+            total = total + part.astype(F32)
+        return total
+
+    def half_copy(i):
+        out = tables[i][3]
+        sems = s_grad.at[2 * i, 0], s_grad.at[2 * i + 1, 0]
+        return remote(out.at[0], out.at[1], *sems, partner_dp)
+
+    def sum_grads(i, out):
+        for side in range(2):
+            grad_copy(i, side).wait_recv()
+        tables[i][3][0] = half_sum(i, 1 - d).astype(BF16)
+        half_copy(i).start()
+        out[d] = half_sum(i, d)
 
     all_cot = cotall[...].reshape(nq * 2 * quarter, width)
-    all_b = ball[:, :, :, 0:width].reshape(nq * 2 * quarter, width)
+    all_b = ball[:, :, :, :, :, 0:width].reshape(nq * 2 * quarter, width)
     gd[...] = dot_tn(ug_ref[...], all_cot).astype(BF16)
-    loop(1, n_ten, lambda k: grad_copy(2, gd, gd_land, k).start())
+    start_relays(2)
     gg[...] = dot_tn(all_b, dgp_ref[...]).astype(BF16)
+    start_relays(0)
+    x_dbs.middle()
     gu[...] = dot_tn(all_b, dup_ref[...]).astype(BF16)
+    start_relays(1)
 
     summed = x_dbs.total()
     dprobs = routed * summed[:, width : width + TAIL]
@@ -597,7 +880,7 @@
     db = summed[:, 0:width] + dot_nt(dlogits, tails)
     w_db = db * ffn_gain
     grad_hidden = (
-        cotall[q, core].astype(F32)
+        cotall[own].astype(F32)
         + inv_two * w_db
         - hidden * inv_two**3 * (jnp.sum(w_db * hidden, axis=-1, keepdims=True) / width)
     )
@@ -610,20 +893,20 @@
 
     loop(1, n_ten, lambda k: spread(dall, s_dall, k).start())
     x_ys.send()
+    start_grads(2)
     one_hot = lax.broadcasted_iota(jnp.int32, (rows, TAIL), 1)
     ones_ffn = jnp.where(one_hot[0:quarter] == 32, 1.0, 0.0).astype(BF16)
     ones_attn = jnp.where(one_hot == 33, 1.0, 0.0).astype(BF16)
     tail_grad = dot_tn(b_own, dlogits) + dot_tn(ffn_gain_rows, ones_ffn)
     loop(1, n_ten, lambda k: spread(dall, s_dall, k).wait_recv())
 
-    loop(1, n_ten, lambda k: grad_copy(0, gg, gg_land, k).start())
     d_attn = dall[...].reshape(rows, width)
 
     def to_rows(grad):
-        return grad.astype(BF16).reshape(nq, 2, 32, grad.shape[1])
+        return grad.astype(BF16).reshape(n_dp, nx, 2, 2, 32, grad.shape[1])
 
     wgo[...] = to_rows(dot_tn(d_attn, o_low))
-    x_wgo = Scatter(nq, q, core, plane, sibling, wgo, wgo_half, wgo_land, s_wgo)
+    x_wgo = PlaneScatter(plane, wgo, wgo_half, wgo_line, wgo_column, wgo_last, l_wgo, s_wgo)
     x_wgo.start()
     do = dot(d_attn, w_out).astype(BF16)
     for t in range(2):
@@ -633,6 +916,7 @@
 
     dq_ref[...] = jnp.zeros_like(dq_ref)
     x_wgo.send()
+    start_grads(0)
 
     def head_backward(i):
         go = dos[i]
@@ -660,27 +944,31 @@
     dq_lin = jnp.concatenate([unrope(dq_ref[0]), unrope(dq_ref[1])], axis=1) * 0.125
     dq_lin = dq_lin.astype(BF16)
     x_dkv.send()
-    start_all([grad_copy(1, gu, gu_land, 1), grad_copy(1, gu, gu_land, n_ten - 1)])
+    x_ys.middle()
+    x_wgo.middle()
     wgq[...] = to_rows(dot_tn(a_low, dq_lin))
-    x_wgq = Scatter(nq, q, core, plane, sibling, wgq, wgq_half, wgq_land, s_wgq)
+    x_wgq = PlaneScatter(plane, wgq, wgq_half, wgq_line, wgq_column, wgq_last, l_wgq, s_wgq)
     x_wgq.start()
-    da = dot_nt(dq_lin, wall[:, :, :, 0:256].reshape(width, 256))
+    da = dot_nt(dq_lin, wall[:, :, :, :, :, 0:256].reshape(width, 256))
     x_wgq.send()
+    sum_grads(2, od_ref)
     grad_kv = x_dkv.total()
     dkv_lin = jnp.concatenate([unrope(grad_kv[:, 0:128]), grad_kv[:, 128:256]], axis=1)
     dkv_lin = dkv_lin.astype(BF16)
-    da = da + dot_nt(dkv_lin, wall[:, :, :, 256:512].reshape(width, 256))
+    da = da + dot_nt(dkv_lin, wall[:, :, :, :, :, 256:512].reshape(width, 256))
     part[1] = da.astype(BF16).reshape(n_ten, quarter, width)
     loop(1, n_ten, lambda k: tensor_copy(1, s_y2, k).start())
-    wgk[:, :, :, 0:256] = to_rows(dot_tn(a_low, dkv_lin))
+    start_grads(1)
+    wgk[:, :, :, :, :, 0:256] = to_rows(dot_tn(a_low, dkv_lin))
     attn_gain_rows = (da * x_ref[...].astype(F32) * inv).astype(BF16)
-    wgk[:, :, :, 256:384] = to_rows(tail_grad + dot_tn(attn_gain_rows, ones_attn))
-    x_wgk = Scatter(nq, q, core, plane, sibling, wgk, wgk_half, wgk_land, s_wgk)
+    wgk[:, :, :, :, :, 256:384] = to_rows(tail_grad + dot_tn(attn_gain_rows, ones_attn))
+    x_wgk = PlaneScatter(plane, wgk, wgk_half, wgk_line, wgk_column, wgk_last, l_wgk, s_wgk)
     x_wgk.start()
 
     hall[r] = (hidden + x_ys.total()).astype(BF16)
     x_wgk.send()
-    loop(1, n_ten, lambda k: spread(hall, s_fin, k).start())
+    x_wgq.middle()
+    sum_grads(0, og_ref)
 
     grad_a = part[1, r].astype(F32)
     for k in range(1, n_ten):
@@ -701,34 +989,10 @@
         return remote(mine, mine, s_fin.at[2, k], s_fin.at[3, k], tensor(k))
 
     loop(1, n_ten, lambda k: spread_ig(k).start())
-    loop(2, n_ten - 1, lambda k: grad_copy(1, gu, gu_land, k).start())
-
-    def reduce_grads(table, land, place, land_place):
-        same = table[place].astype(F32)
-        for k in range(1, n_ten):
-            same = same + land[(k, *land_place)].astype(F32)
-        return same
-
-    sides = ((gg, gg_land, gg_out), (gu, gu_land, gu_out), (gd, gd_land, gd_out))
-    whole = slice(None)
-
-    def half_sum(i, dp):
-        table, land, _ = sides[i]
-        if i == 2:
-            return reduce_grads(table, land, (f_rows(r), d_rows(dp)), (whole, d_rows(dp)))
-        return reduce_grads(table, land, (d_rows(dp), f_rows(r)), (d_rows(dp), whole))
-
-    def half_copy(i):
-        out = sides[i][2]
-        return remote(
-            out.at[0], out.at[1], s_grad.at[2 * i, 0], s_grad.at[2 * i + 1, 0], partner_dp
-        )
-
-    for i, out in ((2, od_ref), (0, og_ref), (1, ou_ref)):
-        loop(1, n_ten, lambda k: grad_copy(i, *sides[i][:2], k).wait_recv())
-        sides[i][2][0] = half_sum(i, 1 - d).astype(BF16)
-        half_copy(i).start()
-        out[d] = half_sum(i, d)
+    loop(1, n_ten, lambda k: spread(hall, s_fin, k).start())
+    x_wgk.middle()
+
+    sum_grads(1, ou_ref)
 
     stores = []
 
@@ -738,7 +1002,7 @@
 
     for i, out, dst in ((2, od_ref, o_wd), (0, og_ref, o_wg), (1, ou_ref, o_wu)):
         half_copy(i).wait_recv()
-        out[1 - d] = sides[i][2][1].astype(F32)
+        out[1 - d] = tables[i][3][1].astype(F32)
         store(out, dst)
 
     loop(1, n_ten, lambda k: spread(hall, s_fin, k).wait_recv())
@@ -790,12 +1054,13 @@
 
     wait_send_all(across_copies())
 
-    def drain_experts(k):
+    for side, k in enumerate(sides_y):
         wait_send_all(own_copies(k))
         wait_send_all(passed_copies(k))
-        wait_send_all(grad_copies(k))
-
-    loop(1, n_ten, drain_experts)
+        wait_send_all(relay_copies(d, 0, side))
+        wait_send_all(relay_copies(1 - d, 6, side))
+        wait_send_all([relay_grad(i, side) for i in range(3)])
+        wait_send_all([grad_copy(i, side) for i in range(3)])
     for i in range(3):
         half_copy(i).wait_send()
 
@@ -803,6 +1068,7 @@
 def call_layer(sizes, xin, cot, seg, rts, gain_a, gain_f, wq, wk, wv, wo, wr, wgi, wui, wdi):
     n_dp, n_ctx, n_ten = sizes
     nj = n_ctx // 2
+    nx = nj // 2
     nq = n_dp * nj
     rows, width = xin.shape
     seq = n_ctx * rows
@@ -823,11 +1089,23 @@
     def sems(*dims):
         return pltpu.SemaphoreType.DMA(dims)
 
+    def table(chunk, columns):
+        return low(n_dp, nx, 2, 2, chunk, columns)
+
+    def summed(chunk, columns):
+        return [
+            table(chunk, columns),
+            low(n_dp, nx, 2, chunk, columns),
+            low(nx, nx, chunk // 2, columns),
+            low(nx, n_dp, 2, chunk // 2, columns),
+            low(nx, chunk, columns),
+        ]
+
     scratch = [
-        low(nq, 2, 32, 640),
-        low(nq, 2, 32, 256),
-        low(nq, 2, quarter, width),
-        low(nq, 2, quarter, width + TAIL),
+        table(32, 640),
+        table(32, 256),
+        table(quarter, width),
+        table(quarter, width + TAIL),
         low(nj, 2, rows, 256),
         low(width, hidden_units),
         low(width, hidden_units),
@@ -853,18 +1131,17 @@
         low(all_rows, hidden_units),
         low(all_rows, hidden_units),
         low(all_rows, hidden_units),
-        low(nq, 2, quarter, width + TAIL),
-        low(nq, quarter, width + TAIL),
-        low(nq, quarter, width + TAIL),
-        low(nq, 2, quarter, width),
-        low(nq, quarter, width),
-        low(nq, quarter, width),
+        *summed(quarter, width + TAIL),
+        *summed(quarter, width),
         low(width, hidden_units),
         low(width, hidden_units),
         low(hidden_units, width),
-        low(n_ten, width, cut),
-        low(n_ten, width, cut),
-        low(n_ten, cut, width),
+        low(2, width, cut),
+        low(2, width, cut),
+        low(2, cut, width),
+        low(2, half_d, cut),
+        low(2, half_d, cut),
+        low(2, cut, half_d),
         low(2, half_d, cut),
         low(2, half_d, cut),
         low(2, cut, half_d),
@@ -873,36 +1150,35 @@
         low(nj, 2, rows, 256),
         low(nj, rows, 256),
         low(nj, rows, 256),
-        low(nq, 2, 32, 256),
-        low(nq, 32, 256),
-        low(nq, 32, 256),
-        low(nq, 2, 32, 256),
-        low(nq, 32, 256),
-        low(nq, 32, 256),
-        low(nq, 2, 32, 384),
-        low(nq, 32, 384),
-        low(nq, 32, 384),
+        *summed(32, 256),
+        *summed(32, 256),
+        *summed(32, 384),
         full(n_ten, 32, TAIL),
-        sems(nq),
-        sems(3),
-        sems(nq),
-        sems(3),
-        sems(nq),
-        sems(3),
-        sems(nq),
-        sems(3),
+        sems(2, nx),
+        sems(4),
+        sems(2, nx),
+        sems(4),
+        sems(2, nx),
+        sems(4),
+        sems(2, nx),
+        sems(4),
         sems(nj),
         sems(3),
-        sems(12, n_ten),
+        sems(12, n_ten + 2),
         sems(2, n_ten),
+        sems(2, nx),
         sems(4),
+        sems(2, nx),
         sems(4),
-        sems(6, n_ten),
+        sems(6, n_ten + 2),
         sems(2, n_ten),
         sems(4),
         sems(2, n_ten),
+        sems(2, nx),
         sems(4),
+        sems(2, nx),
         sems(4),
+        sems(2, nx),
         sems(4),
         sems(6, n_ten),
         sems(5),

time: 152 us -> 138 us (0.908)
  Pallas kernels: 151 us -> 137 us
    pallas_call x1, Pallas kernels: 147 us -> 133 us  [call_layer(): pl.pallas_call(functools.partial(layer, sizes), out_shape=(shape(n_ten, q...]
where the time goes in v4:
time: 138 us
  Pallas kernels  137 us (99%)
    pallas_call x1, Pallas kernels, call_layer(): pl.pallas_call(functools.partial(layer, sizes), out_shape=(shape(n_ten, q...  133 us
    pallas_call x1, Pallas kernels, call_hand_over(): pl.pallas_call(hand_over, out_shape=[jax.ShapeDtypeStruct(a.shape, a.dtyp...  3.78 us

profile of v4, /device:TPU:0, one launch (start us, length us, event | category | flops | bytes accessed | tf_op | source)
XLA Modules:
  0.0 137.6 jit_solution(11653478454393704839)
XLA Ops:
  0.6 133.2 %shard_map.229 = (bf16[4,32,1024]{2,1,0:T(8,128)(2,1)}, f32[4,32,1024]{2,1,0:T(8,128)}, f32[32,256]{1,0:T(8,128)}, f32[32,128]{1,0:T(8,128)}, f32[32,128]{1,0:T(...) custom-call(bf16[128,1024]{1,0:T(8,128)(2,1)} %xin.1, ...), custom_call_target="tpu_custom_call" | custom-call | flops 10468982784 | bytes 8388608 | tf_op jit(solution)/shard_map/pallas_call | solution.py:1189
  133.8 3.8 %shard_map.230 = (bf16[128,1024]{1,0:T(8,128)(2,1)}, f32[128,1024]{1,0:T(8,128)}, f32[32,256]{1,0:T(8,128)}, f32[32,128]{1,0:T(8,128)}, f32[32,128]{1,0:T(8,128)...) custom-call(bf16[128,1024]{1,0:T(8,128)(2,1)} %bitcast.26, ...), custom_call_target="tpu_custom_call" | custom-call | tf_op jit(solution)/shard_map/pallas_call | solution.py:1234

commit v5 on v4

--- a/solution.py
+++ b/solution.py
@@ -653,13 +653,9 @@
     g_cot = PlaneGather(plane, cotall, l_cot, s_cot)
 
     g_wall.forward()
+    start_all(across_copies())
     g_wall.forward_rest()
-    start_all(across_copies())
     g_wall.finish()
-    for k in sides_y:
-        wait_recv_all(own_copies(k))
-    for side in range(2):
-        start_all(relay_copies(d, 0, side))
 
     tails = wall[:, :, :, :, :, 512:640].reshape(width, TAIL)
     gains = tails.astype(F32).T
@@ -676,6 +672,10 @@
     g_kv = Gather(nj, j, core, along, sibling, kv, l_kv, s_kv)
     g_kv.start()
     g_wout.start()
+    for k in sides_y:
+        wait_recv_all(own_copies(k))
+    for side in range(2):
+        start_all(relay_copies(d, 0, side))
 
     numbers = wall[d, :, :, :, :, 512:640].reshape(nj * 64, TAIL).astype(F32)
     held = jnp.where((lane >= 34) & (lane < 38), numbers, 1e9)
@@ -691,12 +691,11 @@
 
     g_kv.forward()
     g_wout.forward()
-    g_wout.forward_rest()
     g_kv.finish()
+    g_cot.start()
     wait_recv_all(across_copies())
     for k in sides_y:
         passed_copy(0, k).start()
-    g_cot.start()
 
     o_ref[...] = jnp.zeros_like(o_ref)
 
@@ -711,6 +710,7 @@
         o_ref[i // 2] += jnp.where(group_of == lax.rem(i, 2), out, 0.0)
 
     loop(0, 4, head_forward)
+    g_wout.forward_rest()
     g_wout.finish()
     o_low = jnp.concatenate([o_ref[0], o_ref[1]], axis=1).astype(BF16)
     w_out = wall_out[...].reshape(width, 256)
@@ -726,6 +726,7 @@
         )
 
     loop(1, n_ten, lambda k: tensor_copy(0, s_y1, k).start())
+    g_cot.forward()
     hidden = x_ref[wide].astype(F32) + part[0, r].astype(F32)
     for k in range(1, n_ten):
         tensor_copy(0, s_y1, k).wait_recv()
@@ -747,9 +748,8 @@
     g_ball.start()
     for k in sides_y:
         start_all([passed_copy(1, k), passed_copy(2, k)])
-    g_cot.forward()
+    g_ball.forward()
     g_cot.forward_rest()
-    g_ball.forward()
     for k in sides_y:
         wait_recv_all(passed_copies(k))
     for side in range(2):
@@ -905,9 +905,6 @@
     def to_rows(grad):
         return grad.astype(BF16).reshape(n_dp, nx, 2, 2, 32, grad.shape[1])
 
-    wgo[...] = to_rows(dot_tn(d_attn, o_low))
-    x_wgo = PlaneScatter(plane, wgo, wgo_half, wgo_line, wgo_column, wgo_last, l_wgo, s_wgo)
-    x_wgo.start()
     do = dot(d_attn, w_out).astype(BF16)
     for t in range(2):
         tile = do[:, 128 * t : 128 * t + 128].astype(F32)
@@ -915,7 +912,6 @@
             dos[2 * t + g] = jnp.where(group_of == g, tile, 0.0).astype(BF16)
 
     dq_ref[...] = jnp.zeros_like(dq_ref)
-    x_wgo.send()
     start_grads(0)
 
     def head_backward(i):
@@ -943,15 +939,19 @@
     a_low = a_ref[...]
     dq_lin = jnp.concatenate([unrope(dq_ref[0]), unrope(dq_ref[1])], axis=1) * 0.125
     dq_lin = dq_lin.astype(BF16)
+    wgo[...] = to_rows(dot_tn(d_attn, o_low))
+    x_wgo = PlaneScatter(plane, wgo, wgo_half, wgo_line, wgo_column, wgo_last, l_wgo, s_wgo)
     x_dkv.send()
+    x_wgo.start()
     x_ys.middle()
-    x_wgo.middle()
     wgq[...] = to_rows(dot_tn(a_low, dq_lin))
     x_wgq = PlaneScatter(plane, wgq, wgq_half, wgq_line, wgq_column, wgq_last, l_wgq, s_wgq)
     x_wgq.start()
+    x_wgo.send()
     da = dot_nt(dq_lin, wall[:, :, :, :, :, 0:256].reshape(width, 256))
     x_wgq.send()
     sum_grads(2, od_ref)
+    x_wgo.middle()
     grad_kv = x_dkv.total()
     dkv_lin = jnp.concatenate([unrope(grad_kv[:, 0:128]), grad_kv[:, 128:256]], axis=1)
     dkv_lin = dkv_lin.astype(BF16)
@@ -967,8 +967,6 @@
 
     hall[r] = (hidden + x_ys.total()).astype(BF16)
     x_wgk.send()
-    x_wgq.middle()
-    sum_grads(0, og_ref)
 
     grad_a = part[1, r].astype(F32)
     for k in range(1, n_ten):
@@ -991,6 +989,8 @@
     loop(1, n_ten, lambda k: spread_ig(k).start())
     loop(1, n_ten, lambda k: spread(hall, s_fin, k).start())
     x_wgk.middle()
+    x_wgq.middle()
+    sum_grads(0, og_ref)
 
     sum_grads(1, ou_ref)
 

time: 138 us -> 133 us (0.964)
  Pallas kernels: 137 us -> 131 us
    pallas_call x1, Pallas kernels: 133 us -> 128 us  [call_layer(): pl.pallas_call(functools.partial(layer, sizes), out_shape=(shape(n_ten, q...]
where the time goes in v5:
time: 133 us; the launch traced here: 132 us
  Pallas kernels  131 us (98%)
    pallas_call x1, Pallas kernels, call_layer(): pl.pallas_call(functools.partial(layer, sizes), out_shape=(shape(n_ten, q...  128 us
    pallas_call x1, Pallas kernels, call_hand_over(): pl.pallas_call(hand_over, out_shape=[jax.ShapeDtypeStruct(a.shape, a.dtyp...  3.78 us

profile of v5, /device:TPU:0, one launch (start us, length us, event | category | flops | bytes accessed | tf_op | source)
XLA Modules:
  0.0 132.1 jit_solution(18276901410190375669)
XLA Ops:
  0.6 127.6 %shard_map.229 = (bf16[4,32,1024]{2,1,0:T(8,128)(2,1)}, f32[4,32,1024]{2,1,0:T(8,128)}, f32[32,256]{1,0:T(8,128)}, f32[32,128]{1,0:T(8,128)}, f32[32,128]{1,0:T(...) custom-call(bf16[128,1024]{1,0:T(8,128)(2,1)} %xin.1, ...), custom_call_target="tpu_custom_call" | custom-call | flops 10468982784 | bytes 8388608 | tf_op jit(solution)/shard_map/pallas_call | solution.py:1189
  128.3 3.8 %shard_map.230 = (bf16[128,1024]{1,0:T(8,128)(2,1)}, f32[128,1024]{1,0:T(8,128)}, f32[32,256]{1,0:T(8,128)}, f32[32,128]{1,0:T(8,128)}, f32[32,128]{1,0:T(8,128)...) custom-call(bf16[128,1024]{1,0:T(8,128)(2,1)} %bitcast.26, ...), custom_call_target="tpu_custom_call" | custom-call | tf_op jit(solution)/shard_map/pallas_call | solution.py:1234

commit v6 on v5

--- a/solution.py
+++ b/solution.py
@@ -120,6 +120,10 @@
             self.sibling,
         )
 
+    def start_part(self, place):
+        away, half = self.parts.at[place, 1 - self.core], self.half.at[place]
+        remote(away, half, self.sems.at[0], self.sems.at[1], self.sibling).start()
+
     def start(self):
         self.near().start()
 
@@ -256,6 +260,11 @@
         p = self.plane
         away = self.parts.at[:, :, :, 1 - p.core]
         return remote(away, self.half, self.sems.at[2], self.sems.at[3], p.sibling)
+
+    def start_part(self, d, xs):
+        p = self.plane
+        away, half = self.parts.at[d, xs, :, 1 - p.core], self.half.at[d, xs]
+        remote(away, half, self.sems.at[2], self.sems.at[3], p.sibling).start()
 
     def start(self):
         self.near().start()
@@ -776,6 +785,8 @@
     def rows_of(i):
         return pl.ds(pl.multiple_of(i * block, block), block)
 
+    x_dbs = PlaneScatter(plane, dbs, dbs_half, dbs_line, dbs_column, dbs_last, l_dbs, s_dbs)
+
     def expert_block(i):
         b = tokens(ball, i, 0, width)
         packed = tokens(ball, i, width, width + TAIL).astype(F32)
@@ -798,19 +809,11 @@
         dbs[(*place_of(i), slice(width, width + TAIL))] = (
             jnp.where(lane == expert, dgate, 0.0).astype(BF16).reshape(2, 2, 2, quarter, TAIL)
         )
+        x_dbs.start_part(*place_of(i)[:2])
 
     loop(0, steps, expert_block)
-    x_dbs = PlaneScatter(plane, dbs, dbs_half, dbs_line, dbs_column, dbs_last, l_dbs, s_dbs)
-    x_dbs.start()
-
-    def down_block(i):
-        y = dot(ug_ref[rows_of(i)], wd[...])
-        ys[place_of(i)] = y.astype(BF16).reshape(2, 2, 2, quarter, width)
-
-    loop(0, steps, down_block)
+
     x_dbs.send()
-    x_ys = PlaneScatter(plane, ys, ys_half, ys_line, ys_column, ys_last, l_ys, s_ys)
-    x_ys.start()
 
     tables = ((gg, gg_land, gg_relay, gg_out), (gu, gu_land, gu_relay, gu_out), (gd, gd_land, gd_relay, gd_out))
 
@@ -867,6 +870,14 @@
     all_b = ball[:, :, :, :, :, 0:width].reshape(nq * 2 * quarter, width)
     gd[...] = dot_tn(ug_ref[...], all_cot).astype(BF16)
     start_relays(2)
+
+    def down_block(i):
+        y = dot(ug_ref[rows_of(i)], wd[...])
+        ys[place_of(i)] = y.astype(BF16).reshape(2, 2, 2, quarter, width)
+
+    loop(0, steps, down_block)
+    x_ys = PlaneScatter(plane, ys, ys_half, ys_line, ys_column, ys_last, l_ys, s_ys)
+    x_ys.start()
     gg[...] = dot_tn(all_b, dgp_ref[...]).astype(BF16)
     start_relays(0)
     x_dbs.middle()
@@ -924,6 +935,7 @@
         dq_ref[i // 2] += jnp.where(group_of == lax.rem(i, 2), dq, 0.0)
 
     loop(0, 4, head_backward)
+    x_dkv = Scatter(nj, j, core, along, sibling, dkv, dkv_half, dkv_land, s_dkv)
     all_q = qs[...].reshape(4 * rows, 128)
     all_do = dos[...].reshape(4 * rows, 128)
     for i in range(4):
@@ -933,8 +945,7 @@
         dv = dot_tn(p_ref[:, :, span].reshape(4 * rows, seq // 4), all_do)
         dkv[place, :, :, 0:128] = dk.astype(BF16).reshape(nj // 4, 2, rows, 128)
         dkv[place, :, :, 128:256] = dv.astype(BF16).reshape(nj // 4, 2, rows, 128)
-    x_dkv = Scatter(nj, j, core, along, sibling, dkv, dkv_half, dkv_land, s_dkv)
-    x_dkv.start()
+        x_dkv.start_part(place)
 
     a_low = a_ref[...]
     dq_lin = jnp.concatenate([unrope(dq_ref[0]), unrope(dq_ref[1])], axis=1) * 0.125
@@ -943,6 +954,7 @@
     x_wgo = PlaneScatter(plane, wgo, wgo_half, wgo_line, wgo_column, wgo_last, l_wgo, s_wgo)
     x_dkv.send()
     x_wgo.start()
+    start_grads(1)
     x_ys.middle()
     wgq[...] = to_rows(dot_tn(a_low, dq_lin))
     x_wgq = PlaneScatter(plane, wgq, wgq_half, wgq_line, wgq_column, wgq_last, l_wgq, s_wgq)
@@ -951,6 +963,7 @@
     da = dot_nt(dq_lin, wall[:, :, :, :, :, 0:256].reshape(width, 256))
     x_wgq.send()
     sum_grads(2, od_ref)
+    sum_grads(0, og_ref)
     x_wgo.middle()
     grad_kv = x_dkv.total()
     dkv_lin = jnp.concatenate([unrope(grad_kv[:, 0:128]), grad_kv[:, 128:256]], axis=1)
@@ -958,7 +971,6 @@
     da = da + dot_nt(dkv_lin, wall[:, :, :, :, :, 256:512].reshape(width, 256))
     part[1] = da.astype(BF16).reshape(n_ten, quarter, width)
     loop(1, n_ten, lambda k: tensor_copy(1, s_y2, k).start())
-    start_grads(1)
     wgk[:, :, :, :, :, 0:256] = to_rows(dot_tn(a_low, dkv_lin))
     attn_gain_rows = (da * x_ref[...].astype(F32) * inv).astype(BF16)
     wgk[:, :, :, :, :, 256:384] = to_rows(tail_grad + dot_tn(attn_gain_rows, ones_attn))
@@ -988,11 +1000,9 @@
 
     loop(1, n_ten, lambda k: spread_ig(k).start())
     loop(1, n_ten, lambda k: spread(hall, s_fin, k).start())
+    sum_grads(1, ou_ref)
     x_wgk.middle()
     x_wgq.middle()
-    sum_grads(0, og_ref)
-
-    sum_grads(1, ou_ref)
 
     stores = []
 

time: 133 us -> 130 us (0.977)
  Pallas kernels: 131 us -> 129 us
    pallas_call x1, Pallas kernels: 128 us -> 125 us  [call_layer(): pl.pallas_call(functools.partial(layer, sizes), out_shape=(shape(n_ten, q...]
where the time goes in v6:
time: 130 us
  Pallas kernels  129 us (99%)
    pallas_call x1, Pallas kernels, call_layer(): pl.pallas_call(functools.partial(layer, sizes), out_shape=(shape(n_ten, q...  125 us
    pallas_call x1, Pallas kernels, call_hand_over(): pl.pallas_call(hand_over, out_shape=[jax.ShapeDtypeStruct(a.shape, a.dtyp...  3.78 us

profile of v6, /device:TPU:0, one launch (start us, length us, event | category | flops | bytes accessed | tf_op | source)
XLA Modules:
  0.0 129.6 jit_solution(3627846856490045810)
XLA Ops:
  0.6 125.2 %shard_map.229 = (bf16[4,32,1024]{2,1,0:T(8,128)(2,1)}, f32[4,32,1024]{2,1,0:T(8,128)}, f32[32,256]{1,0:T(8,128)}, f32[32,128]{1,0:T(8,128)}, f32[32,128]{1,0:T(...) custom-call(bf16[128,1024]{1,0:T(8,128)(2,1)} %xin.1, ...), custom_call_target="tpu_custom_call" | custom-call | flops 10468982784 | bytes 8388608 | tf_op jit(solution)/shard_map/pallas_call | solution.py:1199
  125.8 3.8 %shard_map.230 = (bf16[128,1024]{1,0:T(8,128)(2,1)}, f32[128,1024]{1,0:T(8,128)}, f32[32,256]{1,0:T(8,128)}, f32[32,128]{1,0:T(8,128)}, f32[32,128]{1,0:T(8,128)...) custom-call(bf16[128,1024]{1,0:T(8,128)(2,1)} %bitcast.26, ...), custom_call_target="tpu_custom_call" | custom-call | tf_op jit(solution)/shard_map/pallas_call | solution.py:1244
